TPU v7x, 256 devices: a whole 4x4x8 slice. The times are simulated.
256 devices in a mesh: lon: 16 (over y_lo, x, core), lat: 16 (over y_hi, z).
Axes of the slice: x: 4, y: 4 (y_hi: 2, y_lo: 2; y = y_hi * 2 + y_lo), z: 8, core: 2. Of those that a mesh axis runs over, the one named last changes fastest.
Arguments:
- fields: bfloat16 [4, 96, 384, 192], P(None, 'lat', 'lon'), may hold values from -36 to 36
- gain_attn: float32 [192], replicated, may hold values from 0.1 to 1.9
- w_qkv: bfloat16 [192, 576], replicated, may hold values from -0.4375 to 0.4375
- bias: bfloat16 [16, 6, 144, 144], P('lat'), may hold values from -6 to 300
- w_proj: bfloat16 [192, 192], replicated, may hold values from -0.4375 to 0.4375
- gain_mlp: float32 [192], replicated, may hold values from 0.1 to 1.9
- w_up: bfloat16 [192, 768], replicated, may hold values from -0.4375 to 0.4375
- w_down: bfloat16 [768, 192], replicated, may hold values from -0.21875 to 0.21875
- cotangent: bfloat16 [4, 96, 384, 192], P(None, 'lat', 'lon'), may hold values from -6 to 6
Outputs:
- output: bfloat16 [4, 96, 384, 192], P(None, 'lat', 'lon')
- grad_fields: bfloat16 [4, 96, 384, 192], P(None, 'lat', 'lon')
- grad_qkv: float32 [192, 576], replicated
- grad_proj: float32 [192, 192], replicated
- grad_up: float32 [192, 768], replicated
- grad_down: float32 [768, 192], replicated
- grad_gain_attn: float32 [192], replicated
- grad_gain_mlp: float32 [192], replicated
All inputs are finite; a program needn't handle non-finite values.
Results may differ from a plain program's by a relative error of at most 0.019.
Values may be sent and summed in bfloat16 or wider, within the bound.
A program may use at most 64 MiB of HBM per device.

v0:
```python
import functools

import jax
import jax.numpy as jnp
import numpy as np
from jax import lax
from jax.experimental import pallas as pl
from jax.experimental.pallas import tpu as pltpu
from jax.sharding import PartitionSpec as P

WLAT = 6
WLON = 12
WTOK = 144
HEADS = 6
HEAD = 32
LEV = 4
C = 192
FF = 768
TOK = 576
NORM_EPS = 1e-05
MASKED = -1e30

PIECES = ((0, 64), (64, 64), (128, 32), (160, 32))

FLAT = 4096
GAIN_ROW = 3456

F32 = jnp.float32
BF16 = jnp.bfloat16
MESH = pl.DeviceIdType.MESH
VMEM = pl.BlockSpec(memory_space=pltpu.VMEM)


def piece_row(row, col):
    if row >= 3 and col >= 6:
        return (row - 3) * 18 + col - 6
    if col >= 6:
        return 64 + row * 18 + col - 6
    if row >= 3:
        return 128 + (row - 3) * 6 + col
    return 160 + row * 6 + col


def one_hot_tables():
    pack = np.zeros((192, 144), np.float32)
    place = np.zeros((144, 192), np.float32)
    for row in range(6):
        for col in range(24):
            pack[piece_row(row, col), row * 24 + col] = 1.0
            at = (col // WLON) * 72 + row * WLON + col % WLON
            place[at, piece_row((row + 3) % 6, (col + 6) % 24)] = 1.0
    return pack, place


def nn(left, right):
    return lax.dot_general(left, right, (((1,), (0,)), ((), ())), preferred_element_type=F32)


def nt(left, right):
    return lax.dot_general(left, right, (((1,), (1,)), ((), ())), preferred_element_type=F32)


def tn(left, right):
    return lax.dot_general(left, right, (((0,), (0,)), ((), ())), preferred_element_type=F32)


def row_mean(values):
    return jnp.sum(values, axis=-1, keepdims=True) * (1.0 / C)


def normalize(values):
    center = values - row_mean(values)
    inv = lax.rsqrt(row_mean(center * center) + NORM_EPS)
    return center * inv, inv


def norm_back(unit, inv, gain, upstream):
    scaled = upstream * gain
    grad = inv * (scaled - row_mean(scaled) - unit * row_mean(scaled * unit))
    return grad, jnp.sum(upstream * unit, axis=0, keepdims=True)


def head_masks():
    head_of = lax.broadcasted_iota(jnp.int32, (1, C), 1) // HEAD
    return [jnp.where(head_of == h, 1.0, 0.0).astype(BF16) for h in range(HEADS)]


def block_kernel(
    x_ref, ct_ref, bias_ref, ga_ref, wqkv_ref, wproj_ref, gm_ref, wup_ref, wdown_ref,
    out_ref, gx_ref, flat_ref,
    bias32, probs, normed_s, qkv_s, mixed_s, hid_grad_s, nm_s, act_s, gpre_s, gqkv_s, gattn_s,
):
    scale = HEAD ** (-0.5)
    masks = head_masks()
    is_last = lax.axis_index("lat") == lax.axis_size("lat") - 1
    row_half = (lax.broadcasted_iota(jnp.int32, (WTOK, WTOK), 0) // WLON) % WLAT < WLAT // 2
    col_half = (lax.broadcasted_iota(jnp.int32, (WTOK, WTOK), 1) // WLON) % WLAT < WLAT // 2
    cut = jnp.logical_and(row_half != col_half, is_last)
    penalty = jnp.where(cut, MASKED, 0.0)
    for h in range(HEADS):
        rows = slice(h * WTOK, (h + 1) * WTOK)
        bias32[rows, :] = bias_ref[rows, :].astype(F32) + penalty

    ga = ga_ref[...]
    gm = gm_ref[...]
    grad_gain_mlp = jnp.zeros((1, C), F32)
    for n in range(4):
        rows = slice(n * WTOK, (n + 1) * WTOK)
        x = x_ref[rows, :].astype(F32)
        unit, _ = normalize(x)
        normed = (unit * ga).astype(BF16)
        normed_s[rows, :] = normed
        qkv = nn(normed, wqkv_ref[...]).astype(BF16)
        qkv_s[rows, :] = qkv
        q = qkv[:, :C]
        k = qkv[:, C:2 * C]
        v = qkv[:, 2 * C:]
        mixed = jnp.zeros((WTOK, C), F32)
        for h in range(HEADS):
            s = nt(q * masks[h], k) * scale + bias32[h * WTOK:(h + 1) * WTOK, :]
            e = jnp.exp(s - jnp.max(s, axis=-1, keepdims=True))
            p = e * (1.0 / jnp.sum(e, axis=-1, keepdims=True))
            probs[n * HEADS + h] = p
            mixed = mixed + nn(p.astype(BF16), v * masks[h])
        mixed = mixed.astype(BF16)
        mixed_s[rows, :] = mixed
        hidden = (x + nn(mixed, wproj_ref[...])).astype(BF16).astype(F32)
        unit, inv = normalize(hidden)
        nm = (unit * gm).astype(BF16)
        nm_s[rows, :] = nm
        ct = ct_ref[rows, :]
        down = jnp.zeros((WTOK, C), F32)
        grad_nm = jnp.zeros((WTOK, C), F32)
        for f in range(3):
            cols = slice(f * 256, (f + 1) * 256)
            z = nn(nm, wup_ref[:, cols])
            phi = 0.5 * (1.0 + lax.erf(z * (0.5 ** 0.5)))
            act = (z * phi).astype(BF16)
            act_s[rows, cols] = act
            slope = phi + z * (jnp.exp(-0.5 * z * z) * ((2 * np.pi) ** -0.5))
            gpre = (nn(ct, wdown_ref[:, cols]) * slope).astype(BF16)
            gpre_s[rows, cols] = gpre
            down = down + nt(act, wdown_ref[:, cols])
            grad_nm = grad_nm + nt(gpre, wup_ref[:, cols])
        out_ref[rows, :] = (hidden + down).astype(BF16)
        grad_h, gain_term = norm_back(unit, inv, gm, grad_nm)
        grad_gain_mlp = grad_gain_mlp + gain_term
        grad_hidden = (ct.astype(F32) + grad_h).astype(BF16)
        hid_grad_s[rows, :] = grad_hidden
        gattn_s[rows, :] = nt(grad_hidden, wproj_ref[...]).astype(BF16)

    def store_blocks(base, values):
        for t in range(values.shape[1] // 128):
            flat_ref[base + t * C:base + (t + 1) * C, :] = values[:, t * 128:(t + 1) * 128].astype(BF16)

    store_blocks(6 * C, tn(nm_s[...], gpre_s[...]))
    store_blocks(12 * C, tn(ct_ref[...], act_s[...]))

    grad_gain_attn = jnp.zeros((1, C), F32)
    for n in range(4):
        rows = slice(n * WTOK, (n + 1) * WTOK)
        qkv = qkv_s[rows, :]
        q = qkv[:, :C]
        k = qkv[:, C:2 * C]
        v = qkv[:, 2 * C:]
        up = gattn_s[rows, :]
        gq = jnp.zeros((WTOK, C), F32)
        gk = jnp.zeros((WTOK, C), F32)
        gv = jnp.zeros((WTOK, C), F32)
        for h in range(HEADS):
            p = probs[n * HEADS + h]
            up_h = up * masks[h]
            gp = nt(up_h, v)
            inner = jnp.sum(p * gp, axis=-1, keepdims=True)
            gs = (p * (gp - inner) * scale).astype(BF16)
            gv = gv + tn(p.astype(BF16), up_h)
            gq = gq + nn(gs, k * masks[h])
            gk = gk + tn(gs, q * masks[h])
        gqkv = jnp.concatenate([gq, gk, gv], axis=1).astype(BF16)
        gqkv_s[rows, :] = gqkv
        grad_rolled = nt(gqkv, wqkv_ref[...]).astype(BF16).astype(F32)
        unit, inv = normalize(x_ref[rows, :].astype(F32))
        grad_x, gain_term = norm_back(unit, inv, ga, grad_rolled)
        grad_gain_attn = grad_gain_attn + gain_term
        gx_ref[rows, :] = (hid_grad_s[rows, :].astype(F32) + grad_x).astype(BF16)

    grad_qkv = tn(normed_s[...], gqkv_s[...])
    grad_proj = tn(mixed_s[...], hid_grad_s[...])
    store_blocks(0, jnp.concatenate([grad_qkv, grad_proj], axis=1))
    row = lax.broadcasted_iota(jnp.int32, (16, 128), 0)
    pad = jnp.zeros((1, 64), F32)
    gains = jnp.zeros((16, 128), F32)
    for g, value in enumerate((grad_gain_attn, grad_gain_mlp)):
        tail = jnp.concatenate([value[:, 128:], pad], axis=1)
        gains = jnp.where(row == 2 * g, value[:, :128], gains)
        gains = jnp.where(row == 2 * g + 1, tail, gains)
    flat_ref[GAIN_ROW:GAIN_ROW + 16, :] = gains.astype(BF16)
    flat_ref[GAIN_ROW + 16:, :] = jnp.zeros((FLAT - GAIN_ROW - 16, 128), BF16)


def block_call(x, ct, bias, gain_attn, w_qkv, w_proj, gain_mlp, w_up, w_down):
    shape = jax.ShapeDtypeStruct
    return pl.pallas_call(
        block_kernel,
        out_shape=(
            shape((TOK, C), BF16),
            shape((TOK, C), BF16),
            shape((FLAT, 128), BF16),
        ),
        in_specs=[VMEM] * 9,
        out_specs=(VMEM,) * 3,
        scratch_shapes=[
            pltpu.VMEM((HEADS * WTOK, WTOK), F32),
            pltpu.VMEM((4 * HEADS, WTOK, WTOK), F32),
            pltpu.VMEM((TOK, C), BF16),
            pltpu.VMEM((TOK, 3 * C), BF16),
            pltpu.VMEM((TOK, C), BF16),
            pltpu.VMEM((TOK, C), BF16),
            pltpu.VMEM((TOK, C), BF16),
            pltpu.VMEM((TOK, FF), BF16),
            pltpu.VMEM((TOK, FF), BF16),
            pltpu.VMEM((TOK, 3 * C), BF16),
            pltpu.VMEM((TOK, C), BF16),
        ],
        compiler_params=pltpu.CompilerParams(vmem_limit_bytes=48 * 2**20),
        name="window_block",
    )(x, ct, bias, gain_attn, w_qkv, w_proj, gain_mlp, w_up, w_down)


def remote(src, dst, send_sem, recv_sem, lon, lat):
    return pltpu.make_async_remote_copy(
        src_ref=src, dst_ref=dst, send_sem=send_sem, recv_sem=recv_sem,
        device_id=(lon, lat), device_id_type=MESH,
    )


def ring(index, step, size):
    return lax.rem(index + step + size, size)


def greet(devices):
    barrier = pltpu.get_barrier_semaphore()
    for device in devices:
        pl.semaphore_signal(barrier, inc=1, device_id=device, device_id_type=MESH)
    pl.semaphore_wait(barrier, len(devices))


def halo_neighbours(lon, lat):
    out = []
    for step in (1, -1):
        out.append((ring(lon, step, 16), lat))
        out.append((lon, ring(lat, step, 16)))
        out.append((ring(lon, step, 16), ring(lat, step, 16)))
    return out


def halo_copies(packed, landed, send_sem, recv_sem, step):
    lon, lat = lax.axis_index("lon"), lax.axis_index("lat")
    far_lon, far_lat = ring(lon, step, 16), ring(lat, step, 16)
    targets = ((lon, far_lat), (far_lon, lat), (far_lon, far_lat))
    copies = []
    for i, (start, size) in enumerate(PIECES[1:]):
        copies.append(remote(
            packed.at[:, pl.ds(start, size), :], landed.at[:, pl.ds(start - 64, size), :],
            send_sem.at[i], recv_sem.at[i], *targets[i],
        ))
    return copies


def halo_in_kernel(
    x_ref, ct_ref, pack_ref, place_ref, xw_ref, ctw_ref, packed, landed, send_sem, recv_sem
):
    lon, lat = lax.axis_index("lon"), lax.axis_index("lat")
    greet(halo_neighbours(lon, lat))
    copies = []
    for a, ref in enumerate((x_ref, ct_ref)):
        for level in range(LEV):
            rows = slice(level * WTOK, (level + 1) * WTOK)
            packed[a, level] = nn(pack_ref[...], ref[rows, :]).astype(BF16)
        mine = halo_copies(packed.at[a], landed.at[a], send_sem.at[a], recv_sem.at[a], -1)
        for copy in mine:
            copy.start()
        copies.append(mine)
    for a, ref in enumerate((xw_ref, ctw_ref)):
        for copy in copies[a]:
            copy.wait()
        for pair in range(LEV // 2):
            grids = []
            for level in (2 * pair, 2 * pair + 1):
                grids.append(
                    nn(place_ref[:, :64], packed[a, level, :64, :])
                    + nn(place_ref[:, 64:], landed[a, level])
                )
            for w in range(2):
                tokens = jnp.concatenate([grid[w * 72:(w + 1) * 72] for grid in grids], axis=0)
                start = (pair * 2 + w) * WTOK
                ref[start:start + WTOK, :] = tokens.astype(BF16)


def halo_in(x, ct, pack, place):
    shape = jax.ShapeDtypeStruct((TOK, C), BF16)
    return pl.pallas_call(
        halo_in_kernel,
        out_shape=(shape, shape),
        in_specs=[VMEM] * 4,
        out_specs=(VMEM, VMEM),
        scratch_shapes=[
            pltpu.VMEM((2, LEV, 192, C), BF16),
            pltpu.VMEM((2, LEV, 128, C), BF16),
            pltpu.SemaphoreType.DMA((2, 3)),
            pltpu.SemaphoreType.DMA((2, 3)),
        ],
        compiler_params=pltpu.CompilerParams(
            collective_id=0, has_side_effects=True, vmem_limit_bytes=24 * 2**20
        ),
        name="halo_in",
    )(x, ct, pack, place)


def pack_back(ref, place_ref, packed):
    for pair in range(LEV // 2):
        windows = []
        for w in range(2):
            start = (pair * 2 + w) * WTOK
            windows.append(ref[start:start + WTOK, :].astype(F32))
        for half in range(2):
            grid = jnp.concatenate([w[half * 72:(half + 1) * 72] for w in windows], axis=0)
            packed[2 * pair + half] = tn(place_ref[...], grid.astype(BF16)).astype(BF16)


def unpack_back(packed, landed, pack_ref, ref):
    for level in range(LEV):
        grid = tn(pack_ref[:64, :], packed[level, :64, :]) + tn(pack_ref[64:, :], landed[level])
        ref[level * WTOK:(level + 1) * WTOK, :] = grid.astype(BF16)


def reduce_kernel(
    out_ref, gx_ref, flat_ref, pack_ref, place_ref,
    out_grid, gx_grid, qkv_ref, proj_ref, up_ref, down_ref, gain_ref,
    packed, landed, halo_send, halo_recv,
    core_in, lon_out, lon_in, lat_out, lat_in, mine_out, full,
    core_send, core_recv, lon_send, lon_recv, lat_send, lat_recv,
    back_send, back_recv, lonb_send, lonb_recv, coreb_send, coreb_recv,
):
    lon, lat = lax.axis_index("lon"), lax.axis_index("lat")
    core, group = lax.rem(lon, 2), lon // 2
    partner = lon + 1 - 2 * core
    half = core * 2048
    devices = halo_neighbours(lon, lat) + [(partner, lat)]
    devices += [(ring(group, k, 8) * 2 + core, lat) for k in range(1, 8)]
    devices += [(lon, ring(lat, k, 16)) for k in range(1, 16)]
    greet(devices)

    def chunk(start, size):
        return pl.ds(pl.multiple_of(start, 16), size)

    started = []

    def start(copy):
        copy.start()
        started.append(copy)
        return copy

    core_copies = []
    for k in range(8):
        rows = chunk(2048 - half + ring(group, k + 1, 8) * 256, 256)
        core_copies.append(start(remote(
            flat_ref.at[rows], core_in.at[k], core_send.at[k], core_recv.at[k], partner, lat
        )))
    halos = []
    for a, ref in enumerate((out_ref, gx_ref)):
        pack_back(ref, place_ref, packed.at[a])
        mine = halo_copies(packed.at[a], landed.at[a], halo_send.at[a], halo_recv.at[a], 1)
        halos.append([start(copy) for copy in mine])
    lon_copies = []
    total = None
    for k in range(8):
        core_copies[k].wait_recv()
        peer = ring(group, k + 1, 8)
        summed = flat_ref[chunk(half + peer * 256, 256), :].astype(F32) + core_in[k].astype(F32)
        if k < 7:
            lon_out[k] = summed.astype(BF16)
            lon_copies.append(start(remote(
                lon_out.at[k], lon_in.at[k], lon_send.at[k], lon_recv.at[k], peer * 2 + core, lat
            )))
        else:
            total = summed
    for k in range(7):
        lon_copies[k].wait_recv()
        total = total + lon_in[k].astype(F32)
    lat_out[...] = total.astype(BF16)
    lat_copies = []
    for k in range(15):
        peer = ring(lat, k + 1, 16)
        lat_copies.append(start(remote(
            lat_out.at[chunk(peer * 16, 16)], lat_in.at[k], lat_send.at[k], lat_recv.at[k], lon, peer
        )))
    total = lat_out[chunk(lat * 16, 16), :].astype(F32)
    for k in range(15):
        lat_copies[k].wait_recv()
        total = total + lat_in[k].astype(F32)
    mine_out[...] = total.astype(BF16)
    base = half + group * 256
    own = chunk(base + lat * 16, 16)
    full[own, :] = mine_out[...]
    back = []
    for k in range(15):
        back.append(start(remote(
            mine_out, full.at[own], back_send.at[k], back_recv.at[k], lon, ring(lat, k + 1, 16)
        )))
    for a, ref in enumerate((out_grid, gx_grid)):
        for copy in halos[a]:
            copy.wait_recv()
        unpack_back(packed.at[a], landed.at[a], pack_ref, ref)
    for copy in back:
        copy.wait_recv()
    rows = chunk(base, 256)
    lon_back = []
    for k in range(7):
        peer = ring(group, k + 1, 8)
        lon_back.append(start(remote(
            full.at[rows], full.at[rows], lonb_send.at[k], lonb_recv.at[k], peer * 2 + core, lat
        )))
    core_back = []
    for k in range(8):
        if k > 0:
            lon_back[k - 1].wait_recv()
        rows = chunk(half + ring(group, -k, 8) * 256, 256)
        core_back.append(start(remote(
            full.at[rows], full.at[rows], coreb_send.at[k], coreb_recv.at[k], partner, lat
        )))
    for copy in core_back:
        copy.wait_recv()
    for copy in started:
        copy.wait_send()

    factor = 1.0 / 384.0

    def block(t):
        return full[t * C:(t + 1) * C, :].astype(F32) * factor

    both = jnp.concatenate([block(t) for t in range(6)], axis=1)
    qkv_ref[...] = both[:, :3 * C]
    proj_ref[...] = both[:, 3 * C:]
    for t in range(6):
        up_ref[:, t * 128:(t + 1) * 128] = block(6 + t)
        down_ref[:, t * 128:(t + 1) * 128] = block(12 + t)
    gains = full[GAIN_ROW:GAIN_ROW + 16, :].astype(F32) * factor
    for g in range(2):
        gain_ref[g:g + 1, :] = jnp.concatenate(
            [gains[2 * g:2 * g + 1], gains[2 * g + 1:2 * g + 2, :64]], axis=1
        )


def reduce_call(out, gx, flat, pack, place):
    shape = jax.ShapeDtypeStruct
    sem = pltpu.SemaphoreType.DMA
    return pl.pallas_call(
        reduce_kernel,
        out_shape=(
            shape((TOK, C), BF16),
            shape((TOK, C), BF16),
            shape((C, 3 * C), F32),
            shape((C, C), F32),
            shape((C, FF), F32),
            shape((C, FF), F32),
            shape((2, C), F32),
        ),
        in_specs=[VMEM] * 5,
        out_specs=(VMEM,) * 7,
        scratch_shapes=[
            pltpu.VMEM((2, LEV, 192, C), BF16),
            pltpu.VMEM((2, LEV, 128, C), BF16),
            sem((2, 3)), sem((2, 3)),
            pltpu.VMEM((8, 256, 128), BF16),
            pltpu.VMEM((7, 256, 128), BF16),
            pltpu.VMEM((7, 256, 128), BF16),
            pltpu.VMEM((256, 128), BF16),
            pltpu.VMEM((15, 16, 128), BF16),
            pltpu.VMEM((16, 128), BF16),
            pltpu.VMEM((FLAT, 128), BF16),
            sem((8,)), sem((8,)), sem((7,)), sem((7,)), sem((15,)), sem((15,)),
            sem((15,)), sem((15,)), sem((7,)), sem((7,)), sem((8,)), sem((8,)),
        ],
        compiler_params=pltpu.CompilerParams(
            collective_id=1, has_side_effects=True, vmem_limit_bytes=32 * 2**20
        ),
        name="reduce_back",
    )(out, gx, flat, pack, place)


def body(fields, gain_attn, w_qkv, bias, w_proj, gain_mlp, w_up, w_down, cotangent):
    pack, place = (jnp.asarray(table, BF16) for table in one_hot_tables())
    x, ct = halo_in(fields.reshape(TOK, C), cotangent.reshape(TOK, C), pack, place)
    out, gx, flat = block_call(
        x, ct, bias.reshape(HEADS * WTOK, WTOK), gain_attn.reshape(1, C), w_qkv, w_proj,
        gain_mlp.reshape(1, C), w_up, w_down.T,
    )
    out, gx, qkv, proj, up, down, gains = reduce_call(out, gx, flat, pack, place)
    return (
        out.reshape(fields.shape), gx.reshape(fields.shape), qkv, proj, up, down.T, gains[0], gains[1]
    )


def solution(mesh):
    grid = P(None, "lat", "lon", None)
    in_specs = (grid, P(), P(), P("lat", None, None, None), P(), P(), P(), P(), grid)
    out_specs = (grid, grid, P(), P(), P(), P(), P(), P())
    return jax.shard_map(body, mesh=mesh, in_specs=in_specs, out_specs=out_specs, check_vma=False)
```

profile of v0, /device:TPU:1, one launch (start us, length us, event | category | flops | bytes accessed | tf_op | source)
XLA Modules:
  0.0 94.4 jit_solution(9476694621149423280)
XLA Ops:
  0.6 0.0 copy-start
  0.6 0.0 copy-start.1
  0.7 0.9 copy-done.1
  1.6 0.0 copy-start.3
  1.6 0.9 copy-done.3
  2.5 0.0 copy-start.5
  2.5 1.0 %copy-done.5 = bf16[4,6,24,192]{3,2,1,0:T(8,128)(2,1)S(1)} copy-done((bf16[4,6,24,192]{3,2,1,0:T(8,128)(2,1)S(1)}, bf16[4,6,24,192]{3,2,1,0:T(8,128)(2,1)}, u32[]{:S(2)}) %copy-start.5) | copy-done | bytes 221208
  3.4 0.0 copy-start.6
  3.4 1.0 %copy-done.6 = bf16[4,6,24,192]{3,2,1,0:T(8,128)(2,1)S(1)} copy-done((bf16[4,6,24,192]{3,2,1,0:T(8,128)(2,1)S(1)}, bf16[4,6,24,192]{3,2,1,0:T(8,128)(2,1)}, u32[]{:S(2)}) %copy-start.6) | copy-done | bytes 221208
  4.4 0.0 copy-start.7
  4.4 0.0 copy-start.12
  4.4 17.2 %halo_in.1 = (bf16[576,192]{1,0:T(8,128)(2,1)S(1)}, bf16[576,192]{1,0:T(8,128)(2,1)S(1)}) custom-call(bf16[576,192]{1,0:T(8,128)(2,1)S(1)} %bitcast.15, bf16[576,192]{1,0:T(8,128)(2,1)S(1)} %bitcast.16, bf16[192,144]{1,0:T(8,128)(2,1)S(1)} %copy-done.1, bf16[144,192]{1,0:T(8,128)(2,1)S(1)} %copy-done.3), custom_call_target="tpu_custom_call" | custom-call | tf_op jit(solution)/shard_map/halo_in/pallas_call | solution.py:302
  21.6 0.0 copy-start.11
  21.6 0.0 copy-done
  21.6 0.0 copy-done.7
  21.7 0.0 copy-done.12
  21.7 0.6 copy-done.11
  22.3 0.0 copy-start.8
  22.3 1.0 %copy-done.8 = bf16[768,192]{0,1:T(8,128)(2,1)S(1)} copy-done((bf16[768,192]{0,1:T(8,128)(2,1)S(1)}, bf16[768,192]{0,1:T(8,128)(2,1)}, u32[]{:S(2)}) %copy-start.8) | copy-done | bytes 294936
  23.3 0.0 copy-start.9
  23.3 0.9 copy-done.9
  24.2 0.0 copy-start.10
  24.2 0.9 copy-done.10
  25.1 0.0 copy-start.2
  25.1 0.0 copy-start.4
  25.1 15.5 %window_block.1 = (bf16[576,192]{1,0:T(8,128)(2,1)S(1)}, bf16[576,192]{1,0:T(8,128)(2,1)S(1)}, bf16[4096,128]{1,0:T(8,128)(2,1)S(1)}) custom-call(bf16[576,192]{1,0:T(8,128)(2,1)S(1)} %get-tuple-element.20.x_ref, bf16[576,192]{1,0:T(8,128)(2,1)S(1)} %get-tuple-element.21.ct_ref, bf16[864,144]{1,0:T(8,128)(2,1)S(1)} %bitcast.12, f32[1,192]{1,0:T(1,128)S(1)} %bitcast.18, ...), custom_call_target="tpu_custom_call" | custom-call | tf_op jit(solution)/shard_map/window_block/pallas_call | solution.py:203
  40.6 0.0 copy-done.2
  40.6 0.0 copy-done.4
  40.6 48.7 %reduce_back.1 = (bf16[576,192]{1,0:T(8,128)(2,1)S(1)}, bf16[576,192]{1,0:T(8,128)(2,1)S(1)}, f32[192,576]{1,0:T(8,128)S(1)}, f32[192,192]{1,0:T(8,128)S(1)}, f3...) custom-call(bf16[576,192]{1,0:T(8,128)(2,1)S(1)} %get-tuple-element.22.out_ref, ...), custom_call_target="tpu_custom_call" | custom-call | tf_op jit(solution)/shard_map/reduce_back/pallas_call | solution.py:458
  89.3 0.6 fusion
  89.9 0.7 copy.25
  90.6 0.7 copy.26
  91.3 0.8 copy.27
  92.1 0.7 copy.28
  92.8 0.8 copy.29
  93.6 0.8 copy.30
Async XLA Ops:
  0.6 21.0 %copy-start = (bf16[1,6,144,144]{3,2,1,0:T(8,128)(2,1)S(1)}, bf16[1,6,144,144]{3,2,1,0:T(8,128)(2,1)}, u32[]{:S(2)}) copy-start(bf16[1,6,144,144]{3,2,1,0:T(8,128)(2,1)} %param.14) | copy-start | bytes 746500
  0.6 0.9 %copy-start.1 = (bf16[192,144]{1,0:T(8,128)(2,1)S(1)}, bf16[192,144]{1,0:T(8,128)(2,1)}, u32[]{:S(2)}) copy-start(bf16[192,144]{1,0:T(8,128)(2,1)} %constant.4.clone.pack_ref) | copy-start | bytes 165892
  1.6 0.9 copy-start.3
  2.5 1.0 %copy-start.5 = (bf16[4,6,24,192]{3,2,1,0:T(8,128)(2,1)S(1)}, bf16[4,6,24,192]{3,2,1,0:T(8,128)(2,1)}, u32[]{:S(2)}) copy-start(bf16[4,6,24,192]{3,2,1,0:T(8,128)(2,1)} %param.11) | copy-start | bytes 663556
  3.4 1.0 %copy-start.6 = (bf16[4,6,24,192]{3,2,1,0:T(8,128)(2,1)S(1)}, bf16[4,6,24,192]{3,2,1,0:T(8,128)(2,1)}, u32[]{:S(2)}) copy-start(bf16[4,6,24,192]{3,2,1,0:T(8,128)(2,1)} %param.19) | copy-start | bytes 663556
  4.4 17.2 %copy-start.7 = (bf16[192,768]{1,0:T(8,128)(2,1)S(1)}, bf16[192,768]{1,0:T(8,128)(2,1)}, u32[]{:S(2)}) copy-start(bf16[192,768]{1,0:T(8,128)(2,1)} %wup_ref.1) | copy-start | bytes 884740
  4.4 17.3 %copy-start.12 = (f32[192]{0:T(256)S(1)}, f32[192]{0:T(256)}, u32[]{:S(2)}) copy-start(f32[192]{0:T(256)} %param.16) | copy-start | bytes 2308
  21.6 0.7 copy-start.11
  22.3 1.0 %copy-start.8 = (bf16[768,192]{0,1:T(8,128)(2,1)S(1)}, bf16[768,192]{0,1:T(8,128)(2,1)}, u32[]{:S(2)}) copy-start(bf16[768,192]{0,1:T(8,128)(2,1)} %param.18) | copy-start | bytes 884740
  23.3 0.9 %copy-start.9 = (bf16[192,576]{1,0:T(8,128)(2,1)S(1)}, bf16[192,576]{1,0:T(8,128)(2,1)}, u32[]{:S(2)}) copy-start(bf16[192,576]{1,0:T(8,128)(2,1)} %wqkv_ref.1) | copy-start | bytes 663556
  24.2 0.9 copy-start.10
  25.1 15.5 %copy-start.2 = (bf16[192,144]{1,0:T(8,128)(2,1)S(1)}, bf16[192,144]{1,0:T(8,128)(2,1)}, u32[]{:S(2)}) copy-start(bf16[192,144]{1,0:T(8,128)(2,1)} %constant.4.clone.pack_ref) | copy-start | bytes 165892
  25.1 15.5 %copy-start.4 = (bf16[144,192]{1,0:T(8,128)(2,1)S(1)}, bf16[144,192]{1,0:T(8,128)(2,1)}, u32[]{:S(2)}) copy-start(bf16[144,192]{1,0:T(8,128)(2,1)} %constant.5.clone.place_ref) | copy-start | bytes 165892
where the time goes:
time: 94.7 us; the launch traced here: 94.4 us
  Pallas kernels  81.4 us (86%)
  local copies, waits for them, and re-layouts  12.3 us (13%)
    pallas_call x1, Pallas kernels, reduce_call(): pl.pallas_call(reduce_kernel, out_shape=(shape((TOK, C), BF16), shape((TO...  48.7 us
    pallas_call x1, Pallas kernels, halo_in(): pl.pallas_call(halo_in_kernel, out_shape=(shape, shape), in_specs=[VMEM]...  17.2 us
    pallas_call x1, Pallas kernels, block_call(): pl.pallas_call(block_kernel, out_shape=(shape((TOK, C), BF16), shape((TOK...  15.5 us
    unnamed x32, local copies, waits for them, and re-layouts  11.7 us

commit v1 on v0

v1 whole, which is shorter than its diff:
```python
import jax
import jax.numpy as jnp
from jax import lax
from jax.experimental import pallas as pl
from jax.experimental.pallas import tpu as pltpu
from jax.sharding import PartitionSpec as P

WLAT = 6
WLON = 12
WTOK = 144
HEADS = 6
HEAD = 32
LEV = 4
C = 192
FF = 768
TOK = 576
NORM_EPS = 1e-05
MASKED = -1e30
FACTOR = 1.0 / 384.0

PIECES = ((0, 64), (64, 64), (128, 32), (160, 32))

CHUNK = (80, 48)
ROWS = (32 * 80, 32 * 48)
GAIN_ROW = 6 * C
PLANE = [(dy, dx) for dy in range(4) for dx in range(4) if (dy, dx) != (0, 0)]

F32 = jnp.float32
BF16 = jnp.bfloat16
MESH = pl.DeviceIdType.MESH
VMEM = pl.BlockSpec(memory_space=pltpu.VMEM)
ANY = pl.BlockSpec(memory_space=pl.ANY)


def nn(left, right):
    return lax.dot_general(left, right, (((1,), (0,)), ((), ())), preferred_element_type=F32)


def nt(left, right):
    return lax.dot_general(left, right, (((1,), (1,)), ((), ())), preferred_element_type=F32)


def tn(left, right):
    return lax.dot_general(left, right, (((0,), (0,)), ((), ())), preferred_element_type=F32)


def row_mean(values):
    return jnp.sum(values, axis=-1, keepdims=True) * (1.0 / C)


def normalize(values):
    center = values - row_mean(values)
    inv = lax.rsqrt(row_mean(center * center) + NORM_EPS)
    return center * inv, inv


def norm_back(unit, inv, gain, upstream):
    scaled = upstream * gain
    grad = inv * (scaled - row_mean(scaled) - unit * row_mean(scaled * unit))
    return grad, jnp.sum(upstream * unit, axis=0, keepdims=True)


def head_masks():
    head_of = lax.broadcasted_iota(jnp.int32, (1, C), 1) // HEAD
    return [jnp.where(head_of == h, 1.0, 0.0).astype(BF16) for h in range(HEADS)]


def piece_row(row, col):
    stay_row = row >= 3
    stay_col = col >= 6
    left = jnp.where(stay_row, 128 + (row - 3) * 6 + col, 160 + row * 6 + col)
    right = jnp.where(stay_row, (row - 3) * 18 + col - 6, 64 + row * 18 + col - 6)
    return jnp.where(stay_col, right, left)


def pack_rows(token):
    return piece_row(token // 24, token % 24)


def place_rows(token):
    window = token // 72
    row = (token % 72) // WLON
    col = token % WLON + window * WLON
    return piece_row((row + 3) % 6, (col + 6) % 24)


def table(rows_of):
    token = lax.broadcasted_iota(jnp.int32, (1, WTOK), 1)
    piece = lax.broadcasted_iota(jnp.int32, (192, WTOK), 0)
    return jnp.where(piece == rows_of(token), 1.0, 0.0).astype(BF16)


def table_t(rows_of):
    token = lax.broadcasted_iota(jnp.int32, (WTOK, 1), 0)
    piece = lax.broadcasted_iota(jnp.int32, (WTOK, 192), 1)
    return jnp.where(piece == rows_of(token), 1.0, 0.0).astype(BF16)


def remote(src, dst, send_sem, recv_sem, device):
    return pltpu.make_async_remote_copy(
        src_ref=src, dst_ref=dst, send_sem=send_sem, recv_sem=recv_sem,
        device_id=device, device_id_type=MESH,
    )


def ring(index, step, size):
    return lax.rem(index + step + size, size)


def chunk(start, size):
    return pl.ds(pl.multiple_of(start, 16), size)


class Place:
    def __init__(self):
        self.lon, self.lat = lax.axis_index("lon"), lax.axis_index("lat")
        self.core = lax.rem(self.lon, 2)
        self.x = lax.rem(self.lon // 2, 4)
        self.y = self.lat // 8 * 2 + self.lon // 8
        self.z = lax.rem(self.lat, 8)

    def device(self, y, x, z, core):
        return ((lax.rem(y, 2) * 4 + x) * 2 + core, y // 2 * 8 + z)

    def other_core(self):
        return self.device(self.y, self.x, self.z, 1 - self.core)

    def plane_spot(self, dy, dx):
        return ring(self.y, dy, 4), ring(self.x, dx, 4)

    def plane_peer(self, dy, dx):
        y, x = self.plane_spot(dy, dx)
        return self.device(y, x, self.z, self.core)

    def z_peer(self, dz):
        return self.device(self.y, self.x, ring(self.z, dz, 8), self.core)

    def halo_targets(self, step):
        lon, lat = ring(self.lon, step, 16), ring(self.lat, step, 16)
        return (self.lon, lat), (lon, self.lat), (lon, lat)

    def everyone(self):
        devices = list(self.halo_targets(1)) + list(self.halo_targets(-1)) + [self.other_core()]
        devices += [self.plane_peer(dy, dx) for dy, dx in PLANE]
        return devices + [self.z_peer(dz) for dz in range(1, 8)]


class Halo:
    def __init__(self, spot, packed, landed, send_sem, recv_sem, step):
        targets = spot.halo_targets(step)
        self.packed, self.landed = packed, landed
        self.copies = [
            remote(
                packed.at[:, pl.ds(start, size), :], landed.at[:, pl.ds(start - 64, size), :],
                send_sem.at[i], recv_sem.at[i], targets[i],
            )
            for i, (start, size) in enumerate(PIECES[1:])
        ]

    def start(self):
        for copy in self.copies:
            copy.start()

    def wait(self):
        for copy in self.copies:
            copy.wait()

    def pack_grid(self, ref, pack_ref):
        for level in range(LEV):
            rows = slice(level * WTOK, (level + 1) * WTOK)
            self.packed[level] = nn(pack_ref[...], ref[rows, :]).astype(BF16)

    def unpack_windows(self, place_t_ref, ref):
        for pair in range(LEV // 2):
            grids = []
            for level in (2 * pair, 2 * pair + 1):
                grids.append(
                    nn(place_t_ref[:, :64], self.packed[level, :64, :])
                    + nn(place_t_ref[:, 64:], self.landed[level])
                )
            for w in range(2):
                tokens = jnp.concatenate([grid[w * 72:(w + 1) * 72] for grid in grids], axis=0)
                start = (pair * 2 + w) * WTOK
                ref[start:start + WTOK, :] = tokens.astype(BF16)

    def pack_windows(self, ref, place_ref, pair):
        windows = []
        for w in range(2):
            start = (pair * 2 + w) * WTOK
            windows.append(ref[start:start + WTOK, :].astype(F32))
        for half in range(2):
            grid = jnp.concatenate([w[half * 72:(half + 1) * 72] for w in windows], axis=0)
            self.packed[2 * pair + half] = nn(place_ref[...], grid.astype(BF16)).astype(BF16)

    def unpack_grid(self, pack_t_ref, ref):
        for level in range(LEV):
            grid = nn(pack_t_ref[:, :64], self.packed[level, :64, :])
            grid = grid + nn(pack_t_ref[:, 64:], self.landed[level])
            ref[level * WTOK:(level + 1) * WTOK, :] = grid.astype(BF16)


class Sum:
    def __init__(self, spot, size, flat, full, bufs, sems):
        self.spot, self.size, self.flat, self.full = spot, size, flat, full
        self.core_in, self.plane_out, self.plane_in, self.z_buf = bufs
        (self.core_s, self.core_r, self.plane_s, self.plane_r, self.z_s, self.z_r,
         self.back_s, self.back_r, self.last_s, self.last_r) = sems
        self.sent = []
        self.half = spot.core * (16 * size)
        self.own = (spot.y * 4 + spot.x) * size

    def launch(self, copy):
        copy.start()
        self.sent.append(copy)
        return copy

    def rows(self, dy, dx):
        y, x = self.spot.plane_spot(dy, dx)
        return (y * 4 + x) * self.size

    def to_core(self):
        other = 16 * self.size - self.half
        self.core_copy = self.launch(remote(
            self.flat.at[chunk(other, 16 * self.size)], self.core_in,
            self.core_s, self.core_r, self.spot.other_core(),
        ))

    def to_plane(self):
        self.core_copy.wait_recv()
        mine = self.flat[chunk(self.half, 16 * self.size), :].astype(F32)
        self.plane_out[...] = (mine + self.core_in[...].astype(F32)).astype(BF16)
        self.plane_copies = [
            self.launch(remote(
                self.plane_out.at[chunk(self.rows(dy, dx), self.size)], self.plane_in.at[k],
                self.plane_s.at[k], self.plane_r.at[k], self.spot.plane_peer(dy, dx),
            ))
            for k, (dy, dx) in enumerate(PLANE)
        ]

    def to_z(self):
        total = self.plane_out[chunk(self.own, self.size), :].astype(F32)
        for k, copy in enumerate(self.plane_copies):
            copy.wait_recv()
            total = total + self.plane_in[k].astype(F32)
        self.z_buf[self.spot.z] = total.astype(BF16)
        self.z_copies = [
            self.launch(remote(
                self.z_buf.at[self.spot.z], self.z_buf.at[self.spot.z],
                self.z_s.at[dz - 1], self.z_r.at[dz - 1], self.spot.z_peer(dz),
            ))
            for dz in range(1, 8)
        ]

    def back_to_plane(self):
        for copy in self.z_copies:
            copy.wait_recv()
        total = self.z_buf[0].astype(F32)
        for z in range(1, 8):
            total = total + self.z_buf[z].astype(F32)
        own = chunk(self.half + self.own, self.size)
        self.full[own, :] = total.astype(BF16)
        self.back_copies = [
            self.launch(remote(
                self.full.at[own], self.full.at[own],
                self.back_s.at[k], self.back_r.at[k], self.spot.plane_peer(dy, dx),
            ))
            for k, (dy, dx) in enumerate(PLANE)
        ]

    def back_to_core(self):
        self.last_copies = []
        for k in range(16):
            dy, dx = (0, 0)
            if k > 0:
                self.back_copies[k - 1].wait_recv()
                dy, dx = PLANE[k - 1]
            rows = chunk(self.half + self.rows(-dy, -dx), self.size)
            self.last_copies.append(self.launch(remote(
                self.full.at[rows], self.full.at[rows],
                self.last_s.at[k], self.last_r.at[k], self.spot.other_core(),
            )))

    def finish(self):
        for copy in self.last_copies:
            copy.wait_recv()

    def drain(self):
        for copy in self.sent:
            copy.wait_send()


def block_kernel(
    x_hbm, ct_hbm, bias_hbm, ga_hbm, wqkv_hbm, wproj_hbm, gm_hbm, wup_hbm, wdown_hbm,
    out_grid, gx_grid, full0, full1,
    x_in, ct_in, bias_in, ga_in, wqkv_in, wproj_in, gm_in, wup_in, wdown_in, load_sem,
    pack, pack_t, place, place_t,
    x_ref, ct_ref, out_ref, gx_ref, bias32, probs,
    normed_s, qkv_s, mixed_s, hid_s, hid_grad_s, nm_s, act_s, gpre_s, gqkv_s, gattn_s,
    packed, landed, halo_send, halo_recv, flat0, flat1,
    core_in0, plane_out0, plane_in0, z_buf0, core_in1, plane_out1, plane_in1, z_buf1,
    *sems,
):
    spot = Place()
    loads = []
    for i, (src, dst) in enumerate((
        (x_hbm, x_in), (ct_hbm, ct_in), (bias_hbm, bias_in), (ga_hbm, ga_in), (wqkv_hbm, wqkv_in),
        (wproj_hbm, wproj_in), (gm_hbm, gm_in), (wup_hbm, wup_in), (wdown_hbm, wdown_in),
    )):
        loads.append(pltpu.make_async_copy(src, dst, load_sem.at[i]))
        loads[-1].start()
    barrier = pltpu.get_barrier_semaphore()
    devices = spot.everyone()
    for device in devices:
        pl.semaphore_signal(barrier, inc=1, device_id=device, device_id_type=MESH)
    halos = [
        Halo(spot, packed.at[a], landed.at[a], halo_send.at[a], halo_recv.at[a], step)
        for a, step in enumerate((-1, -1, 1, 1))
    ]
    x_halo, ct_halo, out_halo, gx_halo = halos
    sums = [
        Sum(spot, CHUNK[0], flat0, full0, (core_in0, plane_out0, plane_in0, z_buf0), sems[:10]),
        Sum(spot, CHUNK[1], flat1, full1, (core_in1, plane_out1, plane_in1, z_buf1), sems[10:]),
    ]
    mlp_sum, attn_sum = sums

    pack[...] = table(pack_rows)
    loads[0].wait()
    x_halo.pack_grid(x_in, pack)
    pl.semaphore_wait(barrier, len(devices))
    x_halo.start()
    pack_t[...] = table_t(pack_rows)
    place[...] = table(place_rows)
    place_t[...] = table_t(place_rows)
    loads[1].wait()
    ct_halo.pack_grid(ct_in, pack)
    loads[2].wait()
    is_last = spot.lat == lax.axis_size("lat") - 1
    row_half = (lax.broadcasted_iota(jnp.int32, (WTOK, 1), 0) // WLON) % WLAT < WLAT // 2
    col_half = (lax.broadcasted_iota(jnp.int32, (1, WTOK), 1) // WLON) % WLAT < WLAT // 2
    cut = jnp.logical_and(row_half != col_half, is_last)
    penalty = jnp.where(cut, MASKED, 0.0)
    for h in range(HEADS):
        rows = slice(h * WTOK, (h + 1) * WTOK)
        bias32[rows, :] = bias_in[rows, :].astype(F32) + penalty
    for load in loads[3:]:
        load.wait()
    x_halo.wait()
    ct_halo.start()
    x_halo.unpack_windows(place_t, x_ref)

    scale = HEAD ** (-0.5)
    masks = head_masks()
    ga = ga_in[...]
    gm = gm_in[...]
    for n in range(4):
        rows = slice(n * WTOK, (n + 1) * WTOK)
        x = x_ref[rows, :].astype(F32)
        unit, _ = normalize(x)
        normed = (unit * ga).astype(BF16)
        normed_s[rows, :] = normed
        qkv = nn(normed, wqkv_in[...]).astype(BF16)
        qkv_s[rows, :] = qkv
        q = qkv[:, :C]
        k = qkv[:, C:2 * C]
        v = qkv[:, 2 * C:]
        mixed = jnp.zeros((WTOK, C), F32)
        for h in range(HEADS):
            s = nt(q * masks[h], k) * scale + bias32[h * WTOK:(h + 1) * WTOK, :]
            e = jnp.exp(s - jnp.max(s, axis=-1, keepdims=True))
            p = e * (1.0 / jnp.sum(e, axis=-1, keepdims=True))
            probs[n * HEADS + h] = p
            mixed = mixed + nn(p.astype(BF16), v * masks[h])
        mixed = mixed.astype(BF16)
        mixed_s[rows, :] = mixed
        hid_s[rows, :] = (x + nn(mixed, wproj_in[...])).astype(BF16)

    ct_halo.wait()
    ct_halo.unpack_windows(place_t, ct_ref)
    grad_gain_mlp = jnp.zeros((1, C), F32)
    for n in range(4):
        rows = slice(n * WTOK, (n + 1) * WTOK)
        hidden = hid_s[rows, :].astype(F32)
        unit, inv = normalize(hidden)
        nm = (unit * gm).astype(BF16)
        nm_s[rows, :] = nm
        ct = ct_ref[rows, :]
        down = jnp.zeros((WTOK, C), F32)
        grad_nm = jnp.zeros((WTOK, C), F32)
        for f in range(3):
            cols = slice(f * 256, (f + 1) * 256)
            z = nn(nm, wup_in[:, cols])
            phi = 0.5 * (1.0 + lax.erf(z * (0.5 ** 0.5)))
            act = (z * phi).astype(BF16)
            act_s[rows, cols] = act
            slope = phi + z * (jnp.exp(-0.5 * z * z) * 0.3989422804014327)
            gpre = (nn(ct, wdown_in[:, cols]) * slope).astype(BF16)
            gpre_s[rows, cols] = gpre
            down = down + nt(act, wdown_in[:, cols])
            grad_nm = grad_nm + nt(gpre, wup_in[:, cols])
        out_ref[rows, :] = (hidden + down).astype(BF16)
        grad_h, gain_term = norm_back(unit, inv, gm, grad_nm)
        grad_gain_mlp = grad_gain_mlp + gain_term
        grad_hidden = (ct.astype(F32) + grad_h).astype(BF16)
        hid_grad_s[rows, :] = grad_hidden
        gattn_s[rows, :] = nt(grad_hidden, wproj_in[...]).astype(BF16)

    def store_blocks(flat, base, values):
        for t in range(6):
            flat[base + t * C:base + (t + 1) * C, :] = values[:, t * 128:(t + 1) * 128].astype(BF16)

    store_blocks(flat0, 0, tn(nm_s[...], gpre_s[...]))
    store_blocks(flat0, 6 * C, tn(ct_ref[...], act_s[...]))
    flat0[12 * C:, :] = jnp.zeros((ROWS[0] - 12 * C, 128), BF16)
    mlp_sum.to_core()
    for pair in range(2):
        out_halo.pack_windows(out_ref, place, pair)
    out_halo.start()

    grad_gain_attn = jnp.zeros((1, C), F32)
    for n in range(4):
        rows = slice(n * WTOK, (n + 1) * WTOK)
        qkv = qkv_s[rows, :]
        q = qkv[:, :C]
        k = qkv[:, C:2 * C]
        v = qkv[:, 2 * C:]
        up = gattn_s[rows, :]
        gq = jnp.zeros((WTOK, C), F32)
        gk = jnp.zeros((WTOK, C), F32)
        gv = jnp.zeros((WTOK, C), F32)
        for h in range(HEADS):
            p = probs[n * HEADS + h]
            up_h = up * masks[h]
            gp = nt(up_h, v)
            inner = jnp.sum(p * gp, axis=-1, keepdims=True)
            gs = (p * (gp - inner) * scale).astype(BF16)
            gv = gv + tn(p.astype(BF16), up_h)
            gq = gq + nn(gs, k * masks[h])
            gk = gk + tn(gs, q * masks[h])
        gqkv = jnp.concatenate([gq, gk, gv], axis=1).astype(BF16)
        gqkv_s[rows, :] = gqkv
        grad_rolled = nt(gqkv, wqkv_in[...]).astype(BF16).astype(F32)
        unit, inv = normalize(x_ref[rows, :].astype(F32))
        grad_x, gain_term = norm_back(unit, inv, ga, grad_rolled)
        grad_gain_attn = grad_gain_attn + gain_term
        gx_ref[rows, :] = (hid_grad_s[rows, :].astype(F32) + grad_x).astype(BF16)
        if n == 0:
            mlp_sum.to_plane()
    grad_qkv = tn(normed_s[...], gqkv_s[...])
    grad_proj = tn(mixed_s[...], hid_grad_s[...])
    store_blocks(flat1, 0, jnp.concatenate([grad_qkv, grad_proj], axis=1))
    row = lax.broadcasted_iota(jnp.int32, (16, 128), 0)
    pad = jnp.zeros((1, 64), F32)
    gains = jnp.zeros((16, 128), F32)
    for g, value in enumerate((grad_gain_attn, grad_gain_mlp)):
        tail = jnp.concatenate([value[:, 128:], pad], axis=1)
        gains = jnp.where(row == 2 * g, value[:, :128], gains)
        gains = jnp.where(row == 2 * g + 1, tail, gains)
    flat1[GAIN_ROW:GAIN_ROW + 16, :] = gains.astype(BF16)
    flat1[GAIN_ROW + 16:, :] = jnp.zeros((ROWS[1] - GAIN_ROW - 16, 128), BF16)
    attn_sum.to_core()
    mlp_sum.to_z()
    attn_sum.to_plane()
    for pair in range(2):
        gx_halo.pack_windows(gx_ref, place, pair)
    gx_halo.start()
    mlp_sum.back_to_plane()
    attn_sum.to_z()
    out_halo.wait()
    out_halo.unpack_grid(pack_t, out_grid)
    mlp_sum.back_to_core()
    attn_sum.back_to_plane()
    gx_halo.wait()
    gx_halo.unpack_grid(pack_t, gx_grid)
    attn_sum.back_to_core()
    mlp_sum.finish()
    attn_sum.finish()
    mlp_sum.drain()
    attn_sum.drain()


def sum_bufs(size):
    return [
        pltpu.VMEM((16 * size, 128), BF16),
        pltpu.VMEM((16 * size, 128), BF16),
        pltpu.VMEM((15, size, 128), BF16),
        pltpu.VMEM((8, size, 128), BF16),
    ]


def sum_sems():
    sem = pltpu.SemaphoreType.DMA
    one = pltpu.SemaphoreType.DMA
    counts = (15, 15, 7, 7, 15, 15, 16, 16)
    return [one, one] + [sem((count,)) for count in counts]


def block_call(x, ct, bias, gain_attn, w_qkv, w_proj, gain_mlp, w_up, w_down):
    shape = jax.ShapeDtypeStruct
    args = (x, ct, bias, gain_attn, w_qkv, w_proj, gain_mlp, w_up, w_down)
    sem = pltpu.SemaphoreType.DMA
    return pl.pallas_call(
        block_kernel,
        out_shape=(
            shape((TOK, C), BF16),
            shape((TOK, C), BF16),
            shape((ROWS[0], 128), BF16),
            shape((ROWS[1], 128), BF16),
        ),
        in_specs=[ANY] * 9,
        out_specs=(VMEM,) * 4,
        scratch_shapes=[
            *[pltpu.VMEM(arg.shape, arg.dtype) for arg in args], sem((9,)),
            pltpu.VMEM((192, WTOK), BF16),
            pltpu.VMEM((WTOK, 192), BF16),
            pltpu.VMEM((192, WTOK), BF16),
            pltpu.VMEM((WTOK, 192), BF16),
            pltpu.VMEM((TOK, C), BF16),
            pltpu.VMEM((TOK, C), BF16),
            pltpu.VMEM((TOK, C), BF16),
            pltpu.VMEM((TOK, C), BF16),
            pltpu.VMEM((HEADS * WTOK, WTOK), F32),
            pltpu.VMEM((4 * HEADS, WTOK, WTOK), F32),
            pltpu.VMEM((TOK, C), BF16),
            pltpu.VMEM((TOK, 3 * C), BF16),
            pltpu.VMEM((TOK, C), BF16),
            pltpu.VMEM((TOK, C), BF16),
            pltpu.VMEM((TOK, C), BF16),
            pltpu.VMEM((TOK, C), BF16),
            pltpu.VMEM((TOK, FF), BF16),
            pltpu.VMEM((TOK, FF), BF16),
            pltpu.VMEM((TOK, 3 * C), BF16),
            pltpu.VMEM((TOK, C), BF16),
            pltpu.VMEM((4, LEV, 192, C), BF16),
            pltpu.VMEM((4, LEV, 128, C), BF16),
            sem((4, 3)), sem((4, 3)),
            pltpu.VMEM((ROWS[0], 128), BF16),
            pltpu.VMEM((ROWS[1], 128), BF16),
            *sum_bufs(CHUNK[0]), *sum_bufs(CHUNK[1]),
            *sum_sems(), *sum_sems(),
        ],
        compiler_params=pltpu.CompilerParams(
            collective_id=0, has_side_effects=True, vmem_limit_bytes=56 * 2**20
        ),
        name="block",
    )(*args)


def finish_kernel(
    out_in, gx_in, full0, full1, out_ref, gx_ref, qkv_ref, proj_ref, up_ref, down_ref, gain_ref
):
    def block(full, t):
        return full[t * C:(t + 1) * C, :].astype(F32) * FACTOR

    out_ref[...] = out_in[...]
    gx_ref[...] = gx_in[...]
    both = jnp.concatenate([block(full1, t) for t in range(6)], axis=1)
    qkv_ref[...] = both[:, :3 * C]
    proj_ref[...] = both[:, 3 * C:]
    for t in range(6):
        up_ref[:, t * 128:(t + 1) * 128] = block(full0, t)
        down_ref[:, t * 128:(t + 1) * 128] = block(full0, 6 + t)
    gains = full1[GAIN_ROW:GAIN_ROW + 16, :].astype(F32) * FACTOR
    for g in range(2):
        gain_ref[g:g + 1, :] = jnp.concatenate(
            [gains[2 * g:2 * g + 1], gains[2 * g + 1:2 * g + 2, :64]], axis=1
        )


def finish_call(out, gx, full0, full1):
    shape = jax.ShapeDtypeStruct
    return pl.pallas_call(
        finish_kernel,
        out_shape=(
            shape((TOK, C), BF16),
            shape((TOK, C), BF16),
            shape((C, 3 * C), F32),
            shape((C, C), F32),
            shape((C, FF), F32),
            shape((C, FF), F32),
            shape((2, C), F32),
        ),
        in_specs=[VMEM] * 4,
        out_specs=(VMEM,) * 7,
        compiler_params=pltpu.CompilerParams(vmem_limit_bytes=32 * 2**20),
        name="finish",
    )(out, gx, full0, full1)


def body(fields, gain_attn, w_qkv, bias, w_proj, gain_mlp, w_up, w_down, cotangent):
    out, gx, full0, full1 = block_call(
        fields.reshape(TOK, C), cotangent.reshape(TOK, C), bias.reshape(HEADS * WTOK, WTOK),
        gain_attn.reshape(1, C), w_qkv, w_proj, gain_mlp.reshape(1, C), w_up, w_down.T,
    )
    out, gx, qkv, proj, up, down, gains = finish_call(out, gx, full0, full1)
    return (
        out.reshape(fields.shape), gx.reshape(fields.shape), qkv, proj, up, down.T, gains[0], gains[1]
    )


def solution(mesh):
    grid = P(None, "lat", "lon", None)
    in_specs = (grid, P(), P(), P("lat", None, None, None), P(), P(), P(), P(), grid)
    out_specs = (grid, grid, P(), P(), P(), P(), P(), P())
    return jax.shard_map(body, mesh=mesh, in_specs=in_specs, out_specs=out_specs, check_vma=False)
```

time: 94.7 us -> 69.9 us (0.74)
  Pallas kernels: 81.4 us -> 64.4 us
  local copies, waits for them, and re-layouts: 12.3 us -> 4.57 us
    pallas_call x2 -> x1, Pallas kernels: 65.9 us -> 1.48 us  [finish_call(): pl.pallas_call(finish_kernel, out_shape=(shape((TOK, C), BF16), shape((TO...]
    pallas_call x1, Pallas kernels: 15.5 us -> 63 us  [block_call(): pl.pallas_call(block_kernel, out_shape=(shape((TOK, C), BF16), shape((TOK...]
    unnamed x32 -> x8, local copies, waits for them, and re-layouts: 11.7 us -> 4 us
where the time goes in v1:
time: 69.9 us; the launch traced here: 69.7 us
  Pallas kernels  64.4 us (92%)
  local copies, waits for them, and re-layouts  4.57 us (7%)
    pallas_call x1, Pallas kernels, block_call(): pl.pallas_call(block_kernel, out_shape=(shape((TOK, C), BF16), shape((TOK...  63 us
    unnamed x8, local copies, waits for them, and re-layouts  4 us
    pallas_call x1, Pallas kernels, finish_call(): pl.pallas_call(finish_kernel, out_shape=(shape((TOK, C), BF16), shape((TO...  1.48 us

profile of v1, /device:TPU:1, one launch (start us, length us, event | category | flops | bytes accessed | tf_op | source)
XLA Modules:
  0.0 69.7 jit_solution(147221628199190384)
XLA Ops:
  0.6 63.0 %block.1 = (bf16[576,192]{1,0:T(8,128)(2,1)}, bf16[576,192]{1,0:T(8,128)(2,1)}, bf16[2560,128]{1,0:T(8,128)(2,1)}, bf16[1536,128]{1,0:T(8,128)(2,1)}) custom-call(bf16[576,192]{1,0:T(8,128)(2,1)} %bitcast.12, bf16[576,192]{1,0:T(8,128)(2,1)} %bitcast.13, bf16[864,144]{1,0:T(8,128)(2,1)} %bitcast.11, f32[1,192]{1,0:T(1,128)} %bitcast.15, ...), custom_call_target="tpu_custom_call" | custom-call | tf_op jit(solution)/shard_map/block/pallas_call | solution.py:501
  63.6 0.0 copy-start
  63.6 1.1 %copy-done = bf16[2560,128]{1,0:T(8,128)(2,1)S(1)} copy-done((bf16[2560,128]{1,0:T(8,128)(2,1)S(1)}, bf16[2560,128]{1,0:T(8,128)(2,1)}, u32[]{:S(2)}) %copy-start) | copy-done | bytes 655384
  64.7 0.0 copy-start.1
  64.7 1.0 %copy-done.1 = bf16[1536,128]{1,0:T(8,128)(2,1)S(1)} copy-done((bf16[1536,128]{1,0:T(8,128)(2,1)S(1)}, bf16[1536,128]{1,0:T(8,128)(2,1)}, u32[]{:S(2)}) %copy-start.1) | copy-done | bytes 393240
  65.7 0.0 copy-start.2
  65.7 1.0 %copy-done.2 = bf16[576,192]{1,0:T(8,128)(2,1)S(1)} copy-done((bf16[576,192]{1,0:T(8,128)(2,1)S(1)}, bf16[576,192]{1,0:T(8,128)(2,1)}, u32[]{:S(2)}) %copy-start.2) | copy-done | bytes 221208
  66.6 0.0 copy-start.3
  66.6 1.0 %copy-done.3 = bf16[576,192]{1,0:T(8,128)(2,1)S(1)} copy-done((bf16[576,192]{1,0:T(8,128)(2,1)S(1)}, bf16[576,192]{1,0:T(8,128)(2,1)}, u32[]{:S(2)}) %copy-start.3) | copy-done | bytes 221208
  67.6 1.5 %finish.1 = (bf16[576,192]{1,0:T(8,128)(2,1)}, bf16[576,192]{1,0:T(8,128)(2,1)}, f32[192,576]{1,0:T(8,128)}, f32[192,192]{1,0:T(8,128)}, f32[192,768]{1,0:T(8,12...) custom-call(bf16[576,192]{1,0:T(8,128)(2,1)S(1)} %copy-done.2, bf16[576,192]{1,0:T(8,128)(2,1)S(1)} %copy-done.3, ...), custom_call_target="tpu_custom_call" | custom-call | tf_op jit(solution)/shard_map/finish/pallas_call | solution.py:571
  69.1 0.6 fusion
Async XLA Ops:
  63.6 1.1 %copy-start = (bf16[2560,128]{1,0:T(8,128)(2,1)S(1)}, bf16[2560,128]{1,0:T(8,128)(2,1)}, u32[]{:S(2)}) copy-start(bf16[2560,128]{1,0:T(8,128)(2,1)} %get-tuple-element.21.full0) | copy-start | bytes 1966084
  64.7 1.0 %copy-start.1 = (bf16[1536,128]{1,0:T(8,128)(2,1)S(1)}, bf16[1536,128]{1,0:T(8,128)(2,1)}, u32[]{:S(2)}) copy-start(bf16[1536,128]{1,0:T(8,128)(2,1)} %get-tuple-element.22.full1) | copy-start | bytes 1179652
  65.7 1.0 %copy-start.2 = (bf16[576,192]{1,0:T(8,128)(2,1)S(1)}, bf16[576,192]{1,0:T(8,128)(2,1)}, u32[]{:S(2)}) copy-start(bf16[576,192]{1,0:T(8,128)(2,1)} %get-tuple-element.19.out_in) | copy-start | bytes 663556
  66.6 1.0 %copy-start.3 = (bf16[576,192]{1,0:T(8,128)(2,1)S(1)}, bf16[576,192]{1,0:T(8,128)(2,1)}, u32[]{:S(2)}) copy-start(bf16[576,192]{1,0:T(8,128)(2,1)} %get-tuple-element.20.gx_in) | copy-start | bytes 663556

commit v2 on v1

--- a/solution.py
+++ b/solution.py
@@ -10,7 +10,6 @@
 WTOK = 144
 HEADS = 6
 HEAD = 32
-LEV = 4
 C = 192
 FF = 768
 TOK = 576
@@ -18,18 +17,21 @@
 MASKED = -1e30
 FACTOR = 1.0 / 384.0
 
-PIECES = ((0, 64), (64, 64), (128, 32), (160, 32))
-
-CHUNK = (80, 48)
-ROWS = (32 * 80, 32 * 48)
-GAIN_ROW = 6 * C
+STAY = 112
+PACKED = 320
+PIECES = ((112, 112), (224, 48), (272, 48))
+PAIR = 288
+
+CHUNK = (80, 32)
+ROWS = (32 * 80, 32 * 32)
+GAIN_ROW = 5 * C
 PLANE = [(dy, dx) for dy in range(4) for dx in range(4) if (dy, dx) != (0, 0)]
 
 F32 = jnp.float32
 BF16 = jnp.bfloat16
 MESH = pl.DeviceIdType.MESH
 VMEM = pl.BlockSpec(memory_space=pltpu.VMEM)
-ANY = pl.BlockSpec(memory_space=pl.ANY)
+HBM = pl.BlockSpec(memory_space=pltpu.HBM)
 
 
 def nn(left, right):
@@ -65,34 +67,34 @@
     return [jnp.where(head_of == h, 1.0, 0.0).astype(BF16) for h in range(HEADS)]
 
 
-def piece_row(row, col):
+def piece_row(level, row, col):
     stay_row = row >= 3
-    stay_col = col >= 6
-    left = jnp.where(stay_row, 128 + (row - 3) * 6 + col, 160 + row * 6 + col)
-    right = jnp.where(stay_row, (row - 3) * 18 + col - 6, 64 + row * 18 + col - 6)
-    return jnp.where(stay_col, right, left)
+    low = jnp.where(stay_row, row - 3, row)
+    wide = level * 54 + low * 18 + col - 6
+    thin = level * 18 + low * 6 + col
+    right = jnp.where(stay_row, wide, wide + PIECES[0][0])
+    left = jnp.where(stay_row, thin + PIECES[1][0], thin + PIECES[2][0])
+    return jnp.where(col >= 6, right, left)
 
 
 def pack_rows(token):
-    return piece_row(token // 24, token % 24)
+    return piece_row(token // 144, token % 144 // 24, token % 24)
 
 
 def place_rows(token):
-    window = token // 72
-    row = (token % 72) // WLON
-    col = token % WLON + window * WLON
-    return piece_row((row + 3) % 6, (col + 6) % 24)
+    col = token % WLON + token // 144 * WLON
+    return piece_row(token % 144 // 72, (token % 72 // WLON + 3) % 6, (col + 6) % 24)
 
 
 def table(rows_of):
-    token = lax.broadcasted_iota(jnp.int32, (1, WTOK), 1)
-    piece = lax.broadcasted_iota(jnp.int32, (192, WTOK), 0)
+    token = lax.broadcasted_iota(jnp.int32, (1, PAIR), 1)
+    piece = lax.broadcasted_iota(jnp.int32, (PACKED, PAIR), 0)
     return jnp.where(piece == rows_of(token), 1.0, 0.0).astype(BF16)
 
 
 def table_t(rows_of):
-    token = lax.broadcasted_iota(jnp.int32, (WTOK, 1), 0)
-    piece = lax.broadcasted_iota(jnp.int32, (WTOK, 192), 1)
+    token = lax.broadcasted_iota(jnp.int32, (PAIR, 1), 0)
+    piece = lax.broadcasted_iota(jnp.int32, (PAIR, PACKED), 1)
     return jnp.where(piece == rows_of(token), 1.0, 0.0).astype(BF16)
 
 
@@ -151,10 +153,10 @@
         self.packed, self.landed = packed, landed
         self.copies = [
             remote(
-                packed.at[:, pl.ds(start, size), :], landed.at[:, pl.ds(start - 64, size), :],
+                packed.at[pl.ds(start, size), :], landed.at[pl.ds(start - STAY, size), :],
                 send_sem.at[i], recv_sem.at[i], targets[i],
             )
-            for i, (start, size) in enumerate(PIECES[1:])
+            for i, (start, size) in enumerate(PIECES)
         ]
 
     def start(self):
@@ -165,38 +167,15 @@
         for copy in self.copies:
             copy.wait()
 
-    def pack_grid(self, ref, pack_ref):
-        for level in range(LEV):
-            rows = slice(level * WTOK, (level + 1) * WTOK)
-            self.packed[level] = nn(pack_ref[...], ref[rows, :]).astype(BF16)
-
-    def unpack_windows(self, place_t_ref, ref):
-        for pair in range(LEV // 2):
-            grids = []
-            for level in (2 * pair, 2 * pair + 1):
-                grids.append(
-                    nn(place_t_ref[:, :64], self.packed[level, :64, :])
-                    + nn(place_t_ref[:, 64:], self.landed[level])
-                )
-            for w in range(2):
-                tokens = jnp.concatenate([grid[w * 72:(w + 1) * 72] for grid in grids], axis=0)
-                start = (pair * 2 + w) * WTOK
-                ref[start:start + WTOK, :] = tokens.astype(BF16)
-
-    def pack_windows(self, ref, place_ref, pair):
-        windows = []
-        for w in range(2):
-            start = (pair * 2 + w) * WTOK
-            windows.append(ref[start:start + WTOK, :].astype(F32))
-        for half in range(2):
-            grid = jnp.concatenate([w[half * 72:(half + 1) * 72] for w in windows], axis=0)
-            self.packed[2 * pair + half] = nn(place_ref[...], grid.astype(BF16)).astype(BF16)
-
-    def unpack_grid(self, pack_t_ref, ref):
-        for level in range(LEV):
-            grid = nn(pack_t_ref[:, :64], self.packed[level, :64, :])
-            grid = grid + nn(pack_t_ref[:, 64:], self.landed[level])
-            ref[level * WTOK:(level + 1) * WTOK, :] = grid.astype(BF16)
+    def pack(self, ref, table_ref):
+        pairs = [ref[i * PAIR:(i + 1) * PAIR, :].astype(F32) for i in range(2)]
+        both = jnp.concatenate(pairs, axis=1).astype(BF16)
+        self.packed[...] = nn(table_ref[...], both).astype(BF16)
+
+    def unpack(self, table_ref, ref):
+        both = nn(table_ref[:, :STAY], self.packed[:STAY, :]) + nn(table_ref[:, STAY:], self.landed[...])
+        for i in range(2):
+            ref[i * PAIR:(i + 1) * PAIR, :] = both[:, i * C:(i + 1) * C].astype(BF16)
 
 
 class Sum:
@@ -325,14 +304,15 @@
 
     pack[...] = table(pack_rows)
     loads[0].wait()
-    x_halo.pack_grid(x_in, pack)
+    x_halo.pack(x_in, pack)
     pl.semaphore_wait(barrier, len(devices))
     x_halo.start()
     pack_t[...] = table_t(pack_rows)
     place[...] = table(place_rows)
     place_t[...] = table_t(place_rows)
     loads[1].wait()
-    ct_halo.pack_grid(ct_in, pack)
+    ct_halo.pack(ct_in, pack)
+    ct_halo.start()
     loads[2].wait()
     is_last = spot.lat == lax.axis_size("lat") - 1
     row_half = (lax.broadcasted_iota(jnp.int32, (WTOK, 1), 0) // WLON) % WLAT < WLAT // 2
@@ -345,8 +325,7 @@
     for load in loads[3:]:
         load.wait()
     x_halo.wait()
-    ct_halo.start()
-    x_halo.unpack_windows(place_t, x_ref)
+    x_halo.unpack(place_t, x_ref)
 
     scale = HEAD ** (-0.5)
     masks = head_masks()
@@ -375,7 +354,7 @@
         hid_s[rows, :] = (x + nn(mixed, wproj_in[...])).astype(BF16)
 
     ct_halo.wait()
-    ct_halo.unpack_windows(place_t, ct_ref)
+    ct_halo.unpack(place_t, ct_ref)
     grad_gain_mlp = jnp.zeros((1, C), F32)
     for n in range(4):
         rows = slice(n * WTOK, (n + 1) * WTOK)
@@ -405,16 +384,17 @@
         gattn_s[rows, :] = nt(grad_hidden, wproj_in[...]).astype(BF16)
 
     def store_blocks(flat, base, values):
-        for t in range(6):
+        for t in range(values.shape[1] // 128):
             flat[base + t * C:base + (t + 1) * C, :] = values[:, t * 128:(t + 1) * 128].astype(BF16)
 
     store_blocks(flat0, 0, tn(nm_s[...], gpre_s[...]))
     store_blocks(flat0, 6 * C, tn(ct_ref[...], act_s[...]))
-    flat0[12 * C:, :] = jnp.zeros((ROWS[0] - 12 * C, 128), BF16)
+    grad_proj = tn(mixed_s[...], hid_grad_s[...])
+    store_blocks(flat0, 12 * C, grad_proj)
+    flat0[13 * C:, :] = jnp.zeros((ROWS[0] - 13 * C, 128), BF16)
     mlp_sum.to_core()
-    for pair in range(2):
-        out_halo.pack_windows(out_ref, place, pair)
-    out_halo.start()
+    out_halo.pack(out_ref, place)
+    mlp_sum.to_plane()
 
     grad_gain_attn = jnp.zeros((1, C), F32)
     for n in range(4):
@@ -443,11 +423,13 @@
         grad_x, gain_term = norm_back(unit, inv, ga, grad_rolled)
         grad_gain_attn = grad_gain_attn + gain_term
         gx_ref[rows, :] = (hid_grad_s[rows, :].astype(F32) + grad_x).astype(BF16)
-        if n == 0:
-            mlp_sum.to_plane()
+        if n == 1:
+            out_halo.start()
+    mlp_sum.to_z()
     grad_qkv = tn(normed_s[...], gqkv_s[...])
-    grad_proj = tn(mixed_s[...], hid_grad_s[...])
-    store_blocks(flat1, 0, jnp.concatenate([grad_qkv, grad_proj], axis=1))
+    store_blocks(flat1, 0, grad_qkv)
+    mixed_tile = jnp.concatenate([grad_qkv[:, 512:], grad_proj[:, 128:]], axis=1)
+    store_blocks(flat1, 4 * C, mixed_tile)
     row = lax.broadcasted_iota(jnp.int32, (16, 128), 0)
     pad = jnp.zeros((1, 64), F32)
     gains = jnp.zeros((16, 128), F32)
@@ -458,21 +440,19 @@
     flat1[GAIN_ROW:GAIN_ROW + 16, :] = gains.astype(BF16)
     flat1[GAIN_ROW + 16:, :] = jnp.zeros((ROWS[1] - GAIN_ROW - 16, 128), BF16)
     attn_sum.to_core()
-    mlp_sum.to_z()
+    gx_halo.pack(gx_ref, place)
     attn_sum.to_plane()
-    for pair in range(2):
-        gx_halo.pack_windows(gx_ref, place, pair)
     gx_halo.start()
     mlp_sum.back_to_plane()
+    out_halo.wait()
+    out_halo.unpack(pack_t, out_grid)
     attn_sum.to_z()
-    out_halo.wait()
-    out_halo.unpack_grid(pack_t, out_grid)
+    gx_halo.wait()
+    gx_halo.unpack(pack_t, gx_grid)
     mlp_sum.back_to_core()
     attn_sum.back_to_plane()
-    gx_halo.wait()
-    gx_halo.unpack_grid(pack_t, gx_grid)
+    mlp_sum.finish()
     attn_sum.back_to_core()
-    mlp_sum.finish()
     attn_sum.finish()
     mlp_sum.drain()
     attn_sum.drain()
@@ -506,14 +486,14 @@
             shape((ROWS[0], 128), BF16),
             shape((ROWS[1], 128), BF16),
         ),
-        in_specs=[ANY] * 9,
+        in_specs=[HBM] * 9,
         out_specs=(VMEM,) * 4,
         scratch_shapes=[
             *[pltpu.VMEM(arg.shape, arg.dtype) for arg in args], sem((9,)),
-            pltpu.VMEM((192, WTOK), BF16),
-            pltpu.VMEM((WTOK, 192), BF16),
-            pltpu.VMEM((192, WTOK), BF16),
-            pltpu.VMEM((WTOK, 192), BF16),
+            pltpu.VMEM((PACKED, PAIR), BF16),
+            pltpu.VMEM((PAIR, PACKED), BF16),
+            pltpu.VMEM((PACKED, PAIR), BF16),
+            pltpu.VMEM((PAIR, PACKED), BF16),
             pltpu.VMEM((TOK, C), BF16),
             pltpu.VMEM((TOK, C), BF16),
             pltpu.VMEM((TOK, C), BF16),
@@ -530,8 +510,8 @@
             pltpu.VMEM((TOK, FF), BF16),
             pltpu.VMEM((TOK, 3 * C), BF16),
             pltpu.VMEM((TOK, C), BF16),
-            pltpu.VMEM((4, LEV, 192, C), BF16),
-            pltpu.VMEM((4, LEV, 128, C), BF16),
+            pltpu.VMEM((4, PACKED, 2 * C), BF16),
+            pltpu.VMEM((4, PACKED - STAY, 2 * C), BF16),
             sem((4, 3)), sem((4, 3)),
             pltpu.VMEM((ROWS[0], 128), BF16),
             pltpu.VMEM((ROWS[1], 128), BF16),
@@ -546,24 +526,38 @@
 
 
 def finish_kernel(
-    out_in, gx_in, full0, full1, out_ref, gx_ref, qkv_ref, proj_ref, up_ref, down_ref, gain_ref
+    out_hbm, gx_hbm, full0_hbm, full1_hbm,
+    out_ref, gx_ref, qkv_ref, proj_ref, up_ref, down_ref, ga_ref, gm_ref,
+    full0, full1, sem,
 ):
+    copies = []
+    for i, (src, dst) in enumerate((
+        (full1_hbm, full1), (full0_hbm, full0), (out_hbm, out_ref), (gx_hbm, gx_ref),
+    )):
+        copies.append(pltpu.make_async_copy(src, dst, sem.at[i]))
+        copies[-1].start()
+
     def block(full, t):
         return full[t * C:(t + 1) * C, :].astype(F32) * FACTOR
 
-    out_ref[...] = out_in[...]
-    gx_ref[...] = gx_in[...]
-    both = jnp.concatenate([block(full1, t) for t in range(6)], axis=1)
-    qkv_ref[...] = both[:, :3 * C]
-    proj_ref[...] = both[:, 3 * C:]
+    copies[0].wait()
+    copies[1].wait()
+    for t in range(4):
+        qkv_ref[:, t * 128:(t + 1) * 128] = block(full1, t)
+    mixed_tile = block(full1, 4)
+    qkv_ref[:, 512:] = mixed_tile[:, :64]
+    proj_ref[:, :128] = block(full0, 12)
+    proj_ref[:, 128:] = mixed_tile[:, 64:]
     for t in range(6):
         up_ref[:, t * 128:(t + 1) * 128] = block(full0, t)
         down_ref[:, t * 128:(t + 1) * 128] = block(full0, 6 + t)
     gains = full1[GAIN_ROW:GAIN_ROW + 16, :].astype(F32) * FACTOR
-    for g in range(2):
-        gain_ref[g:g + 1, :] = jnp.concatenate(
+    for g, ref in enumerate((ga_ref, gm_ref)):
+        ref[...] = jnp.concatenate(
             [gains[2 * g:2 * g + 1], gains[2 * g + 1:2 * g + 2, :64]], axis=1
         )
+    copies[2].wait()
+    copies[3].wait()
 
 
 def finish_call(out, gx, full0, full1):
@@ -577,11 +571,17 @@
             shape((C, C), F32),
             shape((C, FF), F32),
             shape((C, FF), F32),
-            shape((2, C), F32),
+            shape((1, C), F32),
+            shape((1, C), F32),
         ),
-        in_specs=[VMEM] * 4,
-        out_specs=(VMEM,) * 7,
-        compiler_params=pltpu.CompilerParams(vmem_limit_bytes=32 * 2**20),
+        in_specs=[HBM] * 4,
+        out_specs=(HBM, HBM) + (VMEM,) * 6,
+        scratch_shapes=[
+            pltpu.VMEM((ROWS[0], 128), BF16),
+            pltpu.VMEM((ROWS[1], 128), BF16),
+            pltpu.SemaphoreType.DMA((4,)),
+        ],
+        compiler_params=pltpu.CompilerParams(vmem_limit_bytes=56 * 2**20),
         name="finish",
     )(out, gx, full0, full1)
 
@@ -591,9 +591,10 @@
         fields.reshape(TOK, C), cotangent.reshape(TOK, C), bias.reshape(HEADS * WTOK, WTOK),
         gain_attn.reshape(1, C), w_qkv, w_proj, gain_mlp.reshape(1, C), w_up, w_down.T,
     )
-    out, gx, qkv, proj, up, down, gains = finish_call(out, gx, full0, full1)
+    out, gx, qkv, proj, up, down, ga, gm = finish_call(out, gx, full0, full1)
     return (
-        out.reshape(fields.shape), gx.reshape(fields.shape), qkv, proj, up, down.T, gains[0], gains[1]
+        out.reshape(fields.shape), gx.reshape(fields.shape), qkv, proj, up, down.T,
+        ga.reshape(C), gm.reshape(C),
     )
 
 

time: 69.9 us -> 79 us (1.13)
  Pallas kernels: 64.4 us -> 78.1 us
  local copies, waits for them, and re-layouts: 4.57 us -> 0 us
    pallas_call x1, Pallas kernels: 1.48 us -> 20.2 us  [finish_call(): pl.pallas_call(finish_kernel, out_shape=(shape((TOK, C), BF16), shape((TO...]
    pallas_call x1, Pallas kernels: 63 us -> 57.9 us  [block_call(): pl.pallas_call(block_kernel, out_shape=(shape((TOK, C), BF16), shape((TOK...]
    unnamed x8 -> x0, local copies, waits for them, and re-layouts: 4 us -> none
where the time goes in v2:
time: 79 us; the launch traced here: 78.9 us
  Pallas kernels  78.1 us (99%)
  between operations  0.8 us (1%)
    pallas_call x1, Pallas kernels, block_call(): pl.pallas_call(block_kernel, out_shape=(shape((TOK, C), BF16), shape((TOK...  57.9 us
    pallas_call x1, Pallas kernels, finish_call(): pl.pallas_call(finish_kernel, out_shape=(shape((TOK, C), BF16), shape((TO...  20.2 us

profile of v2, /device:TPU:1, one launch (start us, length us, event | category | flops | bytes accessed | tf_op | source)
XLA Modules:
  0.0 78.9 jit_solution(18354593275137022743)
XLA Ops:
  0.6 57.9 %block.1 = (bf16[576,192]{1,0:T(8,128)(2,1)}, bf16[576,192]{1,0:T(8,128)(2,1)}, bf16[2560,128]{1,0:T(8,128)(2,1)}, bf16[1024,128]{1,0:T(8,128)(2,1)}) custom-call(bf16[576,192]{1,0:T(8,128)(2,1)} %bitcast.12, bf16[576,192]{1,0:T(8,128)(2,1)} %bitcast.13, bf16[864,144]{1,0:T(8,128)(2,1)} %bitcast.11, f32[1,192]{1,0:T(1,128)} %bitcast.15, ...), custom_call_target="tpu_custom_call" | custom-call | tf_op jit(solution)/shard_map/block/pallas_call | solution.py:481
  58.5 20.2 %finish.1 = (bf16[576,192]{1,0:T(8,128)(2,1)}, bf16[576,192]{1,0:T(8,128)(2,1)}, f32[192,576]{1,0:T(8,128)}, f32[192,192]{1,0:T(8,128)}, f32[192,768]{1,0:T(8,12...) custom-call(bf16[576,192]{1,0:T(8,128)(2,1)} %get-tuple-element.20.out_hbm, ...), custom_call_target="tpu_custom_call" | custom-call | tf_op jit(solution)/shard_map/finish/pallas_call | solution.py:565

commit v3 on v2

--- a/solution.py
+++ b/solution.py
@@ -24,7 +24,6 @@
 
 CHUNK = (80, 32)
 ROWS = (32 * 80, 32 * 32)
-GAIN_ROW = 5 * C
 PLANE = [(dy, dx) for dy in range(4) for dx in range(4) if (dy, dx) != (0, 0)]
 
 F32 = jnp.float32
@@ -59,7 +58,7 @@
 def norm_back(unit, inv, gain, upstream):
     scaled = upstream * gain
     grad = inv * (scaled - row_mean(scaled) - unit * row_mean(scaled * unit))
-    return grad, jnp.sum(upstream * unit, axis=0, keepdims=True)
+    return grad
 
 
 def head_masks():
@@ -308,6 +307,8 @@
     pl.semaphore_wait(barrier, len(devices))
     x_halo.start()
     pack_t[...] = table_t(pack_rows)
+    flat0[13 * C:, :] = jnp.zeros((ROWS[0] - 13 * C, 128), BF16)
+    flat1[5 * C:, :] = jnp.zeros((ROWS[1] - 5 * C, 128), BF16)
     place[...] = table(place_rows)
     place_t[...] = table_t(place_rows)
     loads[1].wait()
@@ -321,7 +322,7 @@
     penalty = jnp.where(cut, MASKED, 0.0)
     for h in range(HEADS):
         rows = slice(h * WTOK, (h + 1) * WTOK)
-        bias32[rows, :] = bias_in[rows, :].astype(F32) + penalty
+        bias32[rows, :] = bias_in[rows, :].astype(F32).T + penalty
     for load in loads[3:]:
         load.wait()
     x_halo.wait()
@@ -331,128 +332,116 @@
     masks = head_masks()
     ga = ga_in[...]
     gm = gm_in[...]
-    for n in range(4):
-        rows = slice(n * WTOK, (n + 1) * WTOK)
-        x = x_ref[rows, :].astype(F32)
+
+    def forward():
+        x = x_ref[...].astype(F32)
         unit, _ = normalize(x)
-        normed = (unit * ga).astype(BF16)
-        normed_s[rows, :] = normed
-        qkv = nn(normed, wqkv_in[...]).astype(BF16)
-        qkv_s[rows, :] = qkv
-        q = qkv[:, :C]
-        k = qkv[:, C:2 * C]
-        v = qkv[:, 2 * C:]
-        mixed = jnp.zeros((WTOK, C), F32)
-        for h in range(HEADS):
-            s = nt(q * masks[h], k) * scale + bias32[h * WTOK:(h + 1) * WTOK, :]
-            e = jnp.exp(s - jnp.max(s, axis=-1, keepdims=True))
-            p = e * (1.0 / jnp.sum(e, axis=-1, keepdims=True))
-            probs[n * HEADS + h] = p
-            mixed = mixed + nn(p.astype(BF16), v * masks[h])
-        mixed = mixed.astype(BF16)
-        mixed_s[rows, :] = mixed
-        hid_s[rows, :] = (x + nn(mixed, wproj_in[...])).astype(BF16)
-
-    ct_halo.wait()
-    ct_halo.unpack(place_t, ct_ref)
-    grad_gain_mlp = jnp.zeros((1, C), F32)
-    for n in range(4):
-        rows = slice(n * WTOK, (n + 1) * WTOK)
-        hidden = hid_s[rows, :].astype(F32)
-        unit, inv = normalize(hidden)
-        nm = (unit * gm).astype(BF16)
-        nm_s[rows, :] = nm
-        ct = ct_ref[rows, :]
-        down = jnp.zeros((WTOK, C), F32)
-        grad_nm = jnp.zeros((WTOK, C), F32)
+        normed_s[...] = (unit * ga).astype(BF16)
+        qkv_s[...] = nn(normed_s[...], wqkv_in[...]).astype(BF16)
+        for n in range(4):
+            rows = slice(n * WTOK, (n + 1) * WTOK)
+            q, k, v = split_heads(rows)
+            km = jnp.concatenate([k * masks[h] for h in range(HEADS)], axis=0)
+            vm = jnp.concatenate([v * masks[h] for h in range(HEADS)], axis=0)
+            s = (nt(km, q) * scale + bias32[...]).reshape(HEADS, WTOK, WTOK)
+            e = jnp.exp(s - jnp.max(s, axis=1, keepdims=True))
+            p = e * (1.0 / jnp.sum(e, axis=1, keepdims=True))
+            probs[n * HEADS:(n + 1) * HEADS] = p
+            mixed = tn(p.astype(BF16).reshape(HEADS * WTOK, WTOK), vm)
+            mixed_s[rows, :] = mixed.astype(BF16)
+
+    def split_heads(rows):
+        qkv = qkv_s[rows, :]
+        return qkv[:, :C], qkv[:, C:2 * C], qkv[:, 2 * C:]
+
+    def mlp():
+        hidden = (x_ref[...].astype(F32) + nn(mixed_s[...], wproj_in[...])).astype(BF16)
+        hid_s[...] = hidden
+        unit, inv = normalize(hidden.astype(F32))
+        nm_s[...] = (unit * gm).astype(BF16)
+        grad_nm = jnp.zeros((TOK, C), F32)
         for f in range(3):
             cols = slice(f * 256, (f + 1) * 256)
-            z = nn(nm, wup_in[:, cols])
+            z = nn(nm_s[...], wup_in[:, cols])
             phi = 0.5 * (1.0 + lax.erf(z * (0.5 ** 0.5)))
-            act = (z * phi).astype(BF16)
-            act_s[rows, cols] = act
+            act_s[:, cols] = (z * phi).astype(BF16)
             slope = phi + z * (jnp.exp(-0.5 * z * z) * 0.3989422804014327)
-            gpre = (nn(ct, wdown_in[:, cols]) * slope).astype(BF16)
-            gpre_s[rows, cols] = gpre
-            down = down + nt(act, wdown_in[:, cols])
+            gpre = (nn(ct_ref[...], wdown_in[:, cols]) * slope).astype(BF16)
+            gpre_s[:, cols] = gpre
             grad_nm = grad_nm + nt(gpre, wup_in[:, cols])
-        out_ref[rows, :] = (hidden + down).astype(BF16)
-        grad_h, gain_term = norm_back(unit, inv, gm, grad_nm)
-        grad_gain_mlp = grad_gain_mlp + gain_term
-        grad_hidden = (ct.astype(F32) + grad_h).astype(BF16)
-        hid_grad_s[rows, :] = grad_hidden
-        gattn_s[rows, :] = nt(grad_hidden, wproj_in[...]).astype(BF16)
+        grad_hidden = (ct_ref[...].astype(F32) + norm_back(unit, inv, gm, grad_nm)).astype(BF16)
+        hid_grad_s[...] = grad_hidden
+        gattn_s[...] = nt(grad_hidden, wproj_in[...]).astype(BF16)
+
+    def attention_back(n):
+        rows = slice(n * WTOK, (n + 1) * WTOK)
+        q, k, v = split_heads(rows)
+        up = gattn_s[rows, :]
+        km = jnp.concatenate([k * masks[h] for h in range(HEADS)], axis=0)
+        vm = jnp.concatenate([v * masks[h] for h in range(HEADS)], axis=0)
+        p = probs[n * HEADS:(n + 1) * HEADS]
+        gp = nt(vm, up).reshape(HEADS, WTOK, WTOK)
+        inner = jnp.sum(p * gp, axis=1, keepdims=True)
+        gs = (p * (gp - inner) * scale).astype(BF16).reshape(HEADS * WTOK, WTOK)
+        gv_all = nn(p.astype(BF16).reshape(HEADS * WTOK, WTOK), up)
+        gk_all = nn(gs, q)
+        gq = tn(gs, km)
+        gk = jnp.zeros((WTOK, C), F32)
+        gv = jnp.zeros((WTOK, C), F32)
+        for h in range(HEADS):
+            gk = jnp.where(masks[h] > 0, gk_all[h * WTOK:(h + 1) * WTOK], gk)
+            gv = jnp.where(masks[h] > 0, gv_all[h * WTOK:(h + 1) * WTOK], gv)
+        gqkv_s[rows, :] = jnp.concatenate([gq, gk, gv], axis=1).astype(BF16)
+
+    def output():
+        out_ref[...] = (hid_s[...].astype(F32) + nt(act_s[...], wdown_in[...])).astype(BF16)
+
+    def input_grad():
+        grad_rolled = nt(gqkv_s[...], wqkv_in[...]).astype(BF16).astype(F32)
+        unit, inv = normalize(x_ref[...].astype(F32))
+        grad_x = norm_back(unit, inv, ga, grad_rolled)
+        gx_ref[...] = (hid_grad_s[...].astype(F32) + grad_x).astype(BF16)
 
     def store_blocks(flat, base, values):
         for t in range(values.shape[1] // 128):
             flat[base + t * C:base + (t + 1) * C, :] = values[:, t * 128:(t + 1) * 128].astype(BF16)
 
+    forward()
+    ct_halo.wait()
+    ct_halo.unpack(place_t, ct_ref)
+    mlp()
     store_blocks(flat0, 0, tn(nm_s[...], gpre_s[...]))
     store_blocks(flat0, 6 * C, tn(ct_ref[...], act_s[...]))
     grad_proj = tn(mixed_s[...], hid_grad_s[...])
     store_blocks(flat0, 12 * C, grad_proj)
-    flat0[13 * C:, :] = jnp.zeros((ROWS[0] - 13 * C, 128), BF16)
     mlp_sum.to_core()
-    out_halo.pack(out_ref, place)
+    attention_back(0)
+    attention_back(1)
     mlp_sum.to_plane()
-
-    grad_gain_attn = jnp.zeros((1, C), F32)
-    for n in range(4):
-        rows = slice(n * WTOK, (n + 1) * WTOK)
-        qkv = qkv_s[rows, :]
-        q = qkv[:, :C]
-        k = qkv[:, C:2 * C]
-        v = qkv[:, 2 * C:]
-        up = gattn_s[rows, :]
-        gq = jnp.zeros((WTOK, C), F32)
-        gk = jnp.zeros((WTOK, C), F32)
-        gv = jnp.zeros((WTOK, C), F32)
-        for h in range(HEADS):
-            p = probs[n * HEADS + h]
-            up_h = up * masks[h]
-            gp = nt(up_h, v)
-            inner = jnp.sum(p * gp, axis=-1, keepdims=True)
-            gs = (p * (gp - inner) * scale).astype(BF16)
-            gv = gv + tn(p.astype(BF16), up_h)
-            gq = gq + nn(gs, k * masks[h])
-            gk = gk + tn(gs, q * masks[h])
-        gqkv = jnp.concatenate([gq, gk, gv], axis=1).astype(BF16)
-        gqkv_s[rows, :] = gqkv
-        grad_rolled = nt(gqkv, wqkv_in[...]).astype(BF16).astype(F32)
-        unit, inv = normalize(x_ref[rows, :].astype(F32))
-        grad_x, gain_term = norm_back(unit, inv, ga, grad_rolled)
-        grad_gain_attn = grad_gain_attn + gain_term
-        gx_ref[rows, :] = (hid_grad_s[rows, :].astype(F32) + grad_x).astype(BF16)
-        if n == 1:
-            out_halo.start()
-    mlp_sum.to_z()
+    attention_back(2)
+    attention_back(3)
     grad_qkv = tn(normed_s[...], gqkv_s[...])
     store_blocks(flat1, 0, grad_qkv)
-    mixed_tile = jnp.concatenate([grad_qkv[:, 512:], grad_proj[:, 128:]], axis=1)
-    store_blocks(flat1, 4 * C, mixed_tile)
-    row = lax.broadcasted_iota(jnp.int32, (16, 128), 0)
-    pad = jnp.zeros((1, 64), F32)
-    gains = jnp.zeros((16, 128), F32)
-    for g, value in enumerate((grad_gain_attn, grad_gain_mlp)):
-        tail = jnp.concatenate([value[:, 128:], pad], axis=1)
-        gains = jnp.where(row == 2 * g, value[:, :128], gains)
-        gains = jnp.where(row == 2 * g + 1, tail, gains)
-    flat1[GAIN_ROW:GAIN_ROW + 16, :] = gains.astype(BF16)
-    flat1[GAIN_ROW + 16:, :] = jnp.zeros((ROWS[1] - GAIN_ROW - 16, 128), BF16)
+    store_blocks(flat1, 4 * C, jnp.concatenate([grad_qkv[:, 512:], grad_proj[:, 128:]], axis=1))
     attn_sum.to_core()
+    output()
+    out_halo.pack(out_ref, place)
+    attn_sum.to_plane()
+    out_halo.start()
+    input_grad()
     gx_halo.pack(gx_ref, place)
-    attn_sum.to_plane()
     gx_halo.start()
-    mlp_sum.back_to_plane()
+    mlp_sum.to_z()
+    attn_sum.to_z()
     out_halo.wait()
     out_halo.unpack(pack_t, out_grid)
-    attn_sum.to_z()
+    mlp_sum.back_to_plane()
+    attn_sum.back_to_plane()
     gx_halo.wait()
     gx_halo.unpack(pack_t, gx_grid)
     mlp_sum.back_to_core()
-    attn_sum.back_to_plane()
+    attn_sum.back_to_core()
     mlp_sum.finish()
-    attn_sum.back_to_core()
     attn_sum.finish()
     mlp_sum.drain()
     attn_sum.drain()
@@ -526,13 +515,14 @@
 
 
 def finish_kernel(
-    out_hbm, gx_hbm, full0_hbm, full1_hbm,
+    out_hbm, gx_hbm, full0_hbm, full1_hbm, wqkv_hbm, wup_hbm, gain_a_hbm, gain_m_hbm,
     out_ref, gx_ref, qkv_ref, proj_ref, up_ref, down_ref, ga_ref, gm_ref,
-    full0, full1, sem,
+    full0, full1, wqkv, wup, gain_a, gain_m, sem,
 ):
     copies = []
     for i, (src, dst) in enumerate((
-        (full1_hbm, full1), (full0_hbm, full0), (out_hbm, out_ref), (gx_hbm, gx_ref),
+        (full1_hbm, full1), (full0_hbm, full0), (wqkv_hbm, wqkv), (wup_hbm, wup),
+        (gain_a_hbm, gain_a), (gain_m_hbm, gain_m), (out_hbm, out_ref), (gx_hbm, gx_ref),
     )):
         copies.append(pltpu.make_async_copy(src, dst, sem.at[i]))
         copies[-1].start()
@@ -551,16 +541,18 @@
     for t in range(6):
         up_ref[:, t * 128:(t + 1) * 128] = block(full0, t)
         down_ref[:, t * 128:(t + 1) * 128] = block(full0, 6 + t)
-    gains = full1[GAIN_ROW:GAIN_ROW + 16, :].astype(F32) * FACTOR
-    for g, ref in enumerate((ga_ref, gm_ref)):
-        ref[...] = jnp.concatenate(
-            [gains[2 * g:2 * g + 1], gains[2 * g + 1:2 * g + 2, :64]], axis=1
+    for copy in copies[2:]:
+        copy.wait()
+    for weight, grad, gain, ref in ((wqkv, qkv_ref, gain_a, ga_ref), (wup, up_ref, gain_m, gm_ref)):
+        product = weight[...].astype(F32) * grad[...]
+        total = lax.dot_general(
+            jnp.ones((8, product.shape[1]), F32), product, (((1,), (1,)), ((), ())),
+            precision=lax.Precision.HIGHEST, preferred_element_type=F32,
         )
-    copies[2].wait()
-    copies[3].wait()
-
-
-def finish_call(out, gx, full0, full1):
+        ref[...] = total[:1] / gain[...]
+
+
+def finish_call(out, gx, full0, full1, w_qkv, w_up, gain_attn, gain_mlp):
     shape = jax.ShapeDtypeStruct
     return pl.pallas_call(
         finish_kernel,
@@ -574,16 +566,20 @@
             shape((1, C), F32),
             shape((1, C), F32),
         ),
-        in_specs=[HBM] * 4,
-        out_specs=(HBM, HBM) + (VMEM,) * 6,
+        in_specs=[HBM] * 8,
+        out_specs=(VMEM,) * 8,
         scratch_shapes=[
             pltpu.VMEM((ROWS[0], 128), BF16),
             pltpu.VMEM((ROWS[1], 128), BF16),
-            pltpu.SemaphoreType.DMA((4,)),
+            pltpu.VMEM((C, 3 * C), BF16),
+            pltpu.VMEM((C, FF), BF16),
+            pltpu.VMEM((1, C), F32),
+            pltpu.VMEM((1, C), F32),
+            pltpu.SemaphoreType.DMA((8,)),
         ],
         compiler_params=pltpu.CompilerParams(vmem_limit_bytes=56 * 2**20),
         name="finish",
-    )(out, gx, full0, full1)
+    )(out, gx, full0, full1, w_qkv, w_up, gain_attn, gain_mlp)
 
 
 def body(fields, gain_attn, w_qkv, bias, w_proj, gain_mlp, w_up, w_down, cotangent):
@@ -591,7 +587,9 @@
         fields.reshape(TOK, C), cotangent.reshape(TOK, C), bias.reshape(HEADS * WTOK, WTOK),
         gain_attn.reshape(1, C), w_qkv, w_proj, gain_mlp.reshape(1, C), w_up, w_down.T,
     )
-    out, gx, qkv, proj, up, down, ga, gm = finish_call(out, gx, full0, full1)
+    out, gx, qkv, proj, up, down, ga, gm = finish_call(
+        out, gx, full0, full1, w_qkv, w_up, gain_attn.reshape(1, C), gain_mlp.reshape(1, C),
+    )
     return (
         out.reshape(fields.shape), gx.reshape(fields.shape), qkv, proj, up, down.T,
         ga.reshape(C), gm.reshape(C),

time: 79 us -> 57.4 us (0.73)
  Pallas kernels: 78.1 us -> 56.5 us
    pallas_call x1, Pallas kernels: 20.2 us -> 3.21 us  [finish_call(): pl.pallas_call(finish_kernel, out_shape=(shape((TOK, C), BF16), shape((TO...]
    pallas_call x1, Pallas kernels: 57.9 us -> 53.3 us  [block_call(): pl.pallas_call(block_kernel, out_shape=(shape((TOK, C), BF16), shape((TOK...]
where the time goes in v3:
time: 57.4 us; the launch traced here: 57.3 us
  Pallas kernels  56.5 us (98%)
  between operations  0.8 us (1%)
    pallas_call x1, Pallas kernels, block_call(): pl.pallas_call(block_kernel, out_shape=(shape((TOK, C), BF16), shape((TOK...  53.3 us
    pallas_call x1, Pallas kernels, finish_call(): pl.pallas_call(finish_kernel, out_shape=(shape((TOK, C), BF16), shape((TO...  3.21 us

profile of v3, /device:TPU:1, one launch (start us, length us, event | category | flops | bytes accessed | tf_op | source)
XLA Modules:
  0.0 57.3 jit_solution(3591388786723759497)
XLA Ops:
  0.6 53.3 %block.1 = (bf16[576,192]{1,0:T(8,128)(2,1)}, bf16[576,192]{1,0:T(8,128)(2,1)}, bf16[2560,128]{1,0:T(8,128)(2,1)}, bf16[1024,128]{1,0:T(8,128)(2,1)}) custom-call(bf16[576,192]{1,0:T(8,128)(2,1)} %bitcast.12, bf16[576,192]{1,0:T(8,128)(2,1)} %bitcast.13, bf16[864,144]{1,0:T(8,128)(2,1)} %bitcast.11, f32[1,192]{1,0:T(1,128)} %bitcast.15, ...), custom_call_target="tpu_custom_call" | custom-call | tf_op jit(solution)/shard_map/block/pallas_call | solution.py:470
  53.9 3.2 %finish.1 = (bf16[576,192]{1,0:T(8,128)(2,1)}, bf16[576,192]{1,0:T(8,128)(2,1)}, f32[192,576]{1,0:T(8,128)}, f32[192,192]{1,0:T(8,128)}, f32[192,768]{1,0:T(8,12...) custom-call(bf16[576,192]{1,0:T(8,128)(2,1)} %get-tuple-element.20.out_hbm, ...), custom_call_target="tpu_custom_call" | custom-call | tf_op jit(solution)/shard_map/finish/pallas_call | solution.py:557

commit v4 on v3

--- a/solution.py
+++ b/solution.py
@@ -22,9 +22,7 @@
 PIECES = ((112, 112), (224, 48), (272, 48))
 PAIR = 288
 
-CHUNK = (80, 32)
-ROWS = (32 * 80, 32 * 32)
-PLANE = [(dy, dx) for dy in range(4) for dx in range(4) if (dy, dx) != (0, 0)]
+ROWS = (1536, 1024, 1024)
 
 F32 = jnp.float32
 BF16 = jnp.bfloat16
@@ -110,6 +108,14 @@
 
 def chunk(start, size):
     return pl.ds(pl.multiple_of(start, 16), size)
+
+
+def near(steps, size):
+    return sorted(steps, key=lambda step: sum(min(d, n - d) for d, n in zip(step, size)))
+
+
+PLANE = near([(dy, dx) for dy in range(4) for dx in range(4) if (dy, dx) != (0, 0)], (4, 4))
+RING = [dz for dz, in near([(dz,) for dz in range(1, 8)], (8,))]
 
 
 class Place:
@@ -178,85 +184,80 @@
 
 
 class Sum:
-    def __init__(self, spot, size, flat, full, bufs, sems):
-        self.spot, self.size, self.flat, self.full = spot, size, flat, full
-        self.core_in, self.plane_out, self.plane_in, self.z_buf = bufs
-        (self.core_s, self.core_r, self.plane_s, self.plane_r, self.z_s, self.z_r,
-         self.back_s, self.back_r, self.last_s, self.last_r) = sems
+    def __init__(self, spot, flat, full, scratch):
+        self.spot, self.flat, self.full = spot, flat, full
+        (self.core_in, self.out, self.first_in, self.second_in, core, first_s, first_r,
+         second_s, second_r, back_s, back_r, last_s, last_r) = scratch
+        self.core_sems = core.at[0], core.at[1]
+        self.first_sems, self.second_sems = (first_s, first_r), (second_s, second_r)
+        self.back_sems, self.last_sems = (back_s, back_r), (last_s, last_r)
+        self.size = self.first_in.shape[1]
         self.sent = []
-        self.half = spot.core * (16 * size)
-        self.own = (spot.y * 4 + spot.x) * size
-
-    def launch(self, copy):
+        self.count = self.first_in.shape[0] + 1
+        self.half = spot.core * (self.count * self.size)
+        self.own = self.first_index(self.first_steps[-1], True) * self.size
+
+    def launch(self, src, dst, sems, device, index=None):
+        send_sem, recv_sem = sems if index is None else (sems[0].at[index], sems[1].at[index])
+        copy = remote(src, dst, send_sem, recv_sem, device)
         copy.start()
         self.sent.append(copy)
         return copy
 
-    def rows(self, dy, dx):
-        y, x = self.spot.plane_spot(dy, dx)
-        return (y * 4 + x) * self.size
+    def far_first(self, steps, make):
+        copies = [make(k, steps[k]) for k in reversed(range(len(steps)))]
+        return copies[::-1]
 
     def to_core(self):
-        other = 16 * self.size - self.half
-        self.core_copy = self.launch(remote(
-            self.flat.at[chunk(other, 16 * self.size)], self.core_in,
-            self.core_s, self.core_r, self.spot.other_core(),
+        other = self.count * self.size - self.half
+        self.core_copy = self.launch(
+            self.flat.at[chunk(other, self.count * self.size)], self.core_in,
+            self.core_sems, self.spot.other_core(),
+        )
+
+    def to_first(self):
+        self.core_copy.wait_recv()
+        mine = self.flat[chunk(self.half, self.count * self.size), :].astype(F32)
+        self.out[...] = (mine + self.core_in[...].astype(F32)).astype(BF16)
+        self.first_copies = self.far_first(self.first_steps, lambda k, step: self.launch(
+            self.out.at[chunk(self.first_index(step) * self.size, self.size)],
+            self.first_in.at[k], self.first_sems, self.first_peer(step), k,
         ))
 
-    def to_plane(self):
-        self.core_copy.wait_recv()
-        mine = self.flat[chunk(self.half, 16 * self.size), :].astype(F32)
-        self.plane_out[...] = (mine + self.core_in[...].astype(F32)).astype(BF16)
-        self.plane_copies = [
-            self.launch(remote(
-                self.plane_out.at[chunk(self.rows(dy, dx), self.size)], self.plane_in.at[k],
-                self.plane_s.at[k], self.plane_r.at[k], self.spot.plane_peer(dy, dx),
-            ))
-            for k, (dy, dx) in enumerate(PLANE)
-        ]
-
-    def to_z(self):
-        total = self.plane_out[chunk(self.own, self.size), :].astype(F32)
-        for k, copy in enumerate(self.plane_copies):
+    def to_second(self):
+        total = self.out[chunk(self.own, self.size), :].astype(F32)
+        for k, copy in enumerate(self.first_copies):
             copy.wait_recv()
-            total = total + self.plane_in[k].astype(F32)
-        self.z_buf[self.spot.z] = total.astype(BF16)
-        self.z_copies = [
-            self.launch(remote(
-                self.z_buf.at[self.spot.z], self.z_buf.at[self.spot.z],
-                self.z_s.at[dz - 1], self.z_r.at[dz - 1], self.spot.z_peer(dz),
-            ))
-            for dz in range(1, 8)
-        ]
-
-    def back_to_plane(self):
-        for copy in self.z_copies:
+            total = total + self.first_in[k].astype(F32)
+        mine = self.second_in.at[self.second_here()]
+        mine[...] = total.astype(BF16)
+        self.second_copies = self.far_first(self.second_steps, lambda k, step: self.launch(
+            mine, mine, self.second_sems, self.second_peer(step), k,
+        ))
+
+    def back_to_first(self):
+        for copy in self.second_copies:
             copy.wait_recv()
-        total = self.z_buf[0].astype(F32)
-        for z in range(1, 8):
-            total = total + self.z_buf[z].astype(F32)
-        own = chunk(self.half + self.own, self.size)
-        self.full[own, :] = total.astype(BF16)
-        self.back_copies = [
-            self.launch(remote(
-                self.full.at[own], self.full.at[own],
-                self.back_s.at[k], self.back_r.at[k], self.spot.plane_peer(dy, dx),
-            ))
-            for k, (dy, dx) in enumerate(PLANE)
-        ]
+        total = self.second_in[0].astype(F32)
+        for i in range(1, len(self.second_steps) + 1):
+            total = total + self.second_in[i].astype(F32)
+        own = self.full.at[chunk(self.half + self.own, self.size)]
+        own[...] = total.astype(BF16)
+        self.back_copies = self.far_first(self.first_steps, lambda k, step: self.launch(
+            own, own, self.back_sems, self.first_peer(step), k,
+        ))
 
     def back_to_core(self):
         self.last_copies = []
-        for k in range(16):
-            dy, dx = (0, 0)
+        for k in range(self.count):
+            start = self.own
             if k > 0:
                 self.back_copies[k - 1].wait_recv()
-                dy, dx = PLANE[k - 1]
-            rows = chunk(self.half + self.rows(-dy, -dx), self.size)
-            self.last_copies.append(self.launch(remote(
-                self.full.at[rows], self.full.at[rows],
-                self.last_s.at[k], self.last_r.at[k], self.spot.other_core(),
-            )))
+                start = self.first_index(self.first_steps[k - 1], False, -1) * self.size
+            rows = self.full.at[chunk(self.half + start, self.size)]
+            self.last_copies.append(
+                self.launch(rows, rows, self.last_sems, self.spot.other_core(), k)
+            )
 
     def finish(self):
         for copy in self.last_copies:
@@ -267,16 +268,63 @@
             copy.wait_send()
 
 
+class PlaneSum(Sum):
+    first_steps, second_steps = PLANE, RING
+
+    def first_index(self, step, here=False, sign=1):
+        y, x = (self.spot.y, self.spot.x) if here else self.spot.plane_spot(sign * step[0], sign * step[1])
+        return y * 4 + x
+
+    def first_peer(self, step):
+        return self.spot.plane_peer(*step)
+
+    def second_here(self):
+        return self.spot.z
+
+    def second_peer(self, step):
+        return self.spot.z_peer(step)
+
+
+class RingSum(Sum):
+    first_steps, second_steps = RING, PLANE
+
+    def first_index(self, step, here=False, sign=1):
+        return self.spot.z if here else ring(self.spot.z, sign * step, 8)
+
+    def first_peer(self, step):
+        return self.spot.z_peer(step)
+
+    def second_here(self):
+        return self.spot.y * 4 + self.spot.x
+
+    def second_peer(self, step):
+        return self.spot.plane_peer(*step)
+
+
+def sum_scratch(kind, size):
+    first, second = len(kind.first_steps), len(kind.second_steps)
+    sem = pltpu.SemaphoreType.DMA
+    return [
+        pltpu.VMEM(((first + 1) * size, 128), BF16),
+        pltpu.VMEM(((first + 1) * size, 128), BF16),
+        pltpu.VMEM((first, size, 128), BF16),
+        pltpu.VMEM((second + 1, size, 128), BF16),
+        sem((2,)), sem((first,)), sem((first,)), sem((second,)), sem((second,)),
+        sem((first,)), sem((first,)), sem((first + 1,)), sem((first + 1,)),
+    ]
+
+
+PARTS = ((PlaneSum, 48), (RingSum, 64), (PlaneSum, 32))
+
+
 def block_kernel(
     x_hbm, ct_hbm, bias_hbm, ga_hbm, wqkv_hbm, wproj_hbm, gm_hbm, wup_hbm, wdown_hbm,
-    out_grid, gx_grid, full0, full1,
+    out_grid, gx_grid, full0, full1, full2,
     x_in, ct_in, bias_in, ga_in, wqkv_in, wproj_in, gm_in, wup_in, wdown_in, load_sem,
     pack, pack_t, place, place_t,
     x_ref, ct_ref, out_ref, gx_ref, bias32, probs,
     normed_s, qkv_s, mixed_s, hid_s, hid_grad_s, nm_s, act_s, gpre_s, gqkv_s, gattn_s,
-    packed, landed, halo_send, halo_recv, flat0, flat1,
-    core_in0, plane_out0, plane_in0, z_buf0, core_in1, plane_out1, plane_in1, z_buf1,
-    *sems,
+    packed, landed, halo_send, halo_recv, flat0, flat1, flat2, *sum_refs,
 ):
     spot = Place()
     loads = []
@@ -295,11 +343,12 @@
         for a, step in enumerate((-1, -1, 1, 1))
     ]
     x_halo, ct_halo, out_halo, gx_halo = halos
-    sums = [
-        Sum(spot, CHUNK[0], flat0, full0, (core_in0, plane_out0, plane_in0, z_buf0), sems[:10]),
-        Sum(spot, CHUNK[1], flat1, full1, (core_in1, plane_out1, plane_in1, z_buf1), sems[10:]),
-    ]
-    mlp_sum, attn_sum = sums
+    sums = []
+    for i, (kind, _) in enumerate(PARTS):
+        flat, full = ((flat0, full0), (flat1, full1), (flat2, full2))[i]
+        count = len(sum_refs) // len(PARTS)
+        sums.append(kind(spot, flat, full, sum_refs[i * count:(i + 1) * count]))
+    early, late = sums[:2], sums[2]
 
     pack[...] = table(pack_rows)
     loads[0].wait()
@@ -307,8 +356,8 @@
     pl.semaphore_wait(barrier, len(devices))
     x_halo.start()
     pack_t[...] = table_t(pack_rows)
-    flat0[13 * C:, :] = jnp.zeros((ROWS[0] - 13 * C, 128), BF16)
     flat1[5 * C:, :] = jnp.zeros((ROWS[1] - 5 * C, 128), BF16)
+    flat2[5 * C:, :] = jnp.zeros((ROWS[2] - 5 * C, 128), BF16)
     place[...] = table(place_rows)
     place_t[...] = table_t(place_rows)
     loads[1].wait()
@@ -410,57 +459,45 @@
     ct_halo.wait()
     ct_halo.unpack(place_t, ct_ref)
     mlp()
-    store_blocks(flat0, 0, tn(nm_s[...], gpre_s[...]))
-    store_blocks(flat0, 6 * C, tn(ct_ref[...], act_s[...]))
+    grad_up = tn(nm_s[...], gpre_s[...])
     grad_proj = tn(mixed_s[...], hid_grad_s[...])
-    store_blocks(flat0, 12 * C, grad_proj)
-    mlp_sum.to_core()
+    store_blocks(flat1, 0, grad_up[:, :640])
+    store_blocks(flat0, 0, tn(ct_ref[...], act_s[...]))
+    store_blocks(flat0, 6 * C, grad_proj)
+    store_blocks(flat0, 7 * C, grad_up[:, 640:])
+    for part in early:
+        part.to_core()
     attention_back(0)
     attention_back(1)
-    mlp_sum.to_plane()
+    for part in early:
+        part.to_first()
     attention_back(2)
     attention_back(3)
     grad_qkv = tn(normed_s[...], gqkv_s[...])
-    store_blocks(flat1, 0, grad_qkv)
-    store_blocks(flat1, 4 * C, jnp.concatenate([grad_qkv[:, 512:], grad_proj[:, 128:]], axis=1))
-    attn_sum.to_core()
+    store_blocks(flat2, 0, grad_qkv)
+    store_blocks(flat2, 4 * C, jnp.concatenate([grad_qkv[:, 512:], grad_proj[:, 128:]], axis=1))
+    late.to_core()
     output()
     out_halo.pack(out_ref, place)
-    attn_sum.to_plane()
-    out_halo.start()
+    late.to_first()
     input_grad()
     gx_halo.pack(gx_ref, place)
+    out_halo.start()
     gx_halo.start()
-    mlp_sum.to_z()
-    attn_sum.to_z()
+    for part in sums:
+        part.to_second()
     out_halo.wait()
     out_halo.unpack(pack_t, out_grid)
-    mlp_sum.back_to_plane()
-    attn_sum.back_to_plane()
+    for part in sums:
+        part.back_to_first()
     gx_halo.wait()
     gx_halo.unpack(pack_t, gx_grid)
-    mlp_sum.back_to_core()
-    attn_sum.back_to_core()
-    mlp_sum.finish()
-    attn_sum.finish()
-    mlp_sum.drain()
-    attn_sum.drain()
-
-
-def sum_bufs(size):
-    return [
-        pltpu.VMEM((16 * size, 128), BF16),
-        pltpu.VMEM((16 * size, 128), BF16),
-        pltpu.VMEM((15, size, 128), BF16),
-        pltpu.VMEM((8, size, 128), BF16),
-    ]
-
-
-def sum_sems():
-    sem = pltpu.SemaphoreType.DMA
-    one = pltpu.SemaphoreType.DMA
-    counts = (15, 15, 7, 7, 15, 15, 16, 16)
-    return [one, one] + [sem((count,)) for count in counts]
+    for part in sums:
+        part.back_to_core()
+    for part in sums:
+        part.finish()
+    for part in sums:
+        part.drain()
 
 
 def block_call(x, ct, bias, gain_attn, w_qkv, w_proj, gain_mlp, w_up, w_down):
@@ -472,11 +509,10 @@
         out_shape=(
             shape((TOK, C), BF16),
             shape((TOK, C), BF16),
-            shape((ROWS[0], 128), BF16),
-            shape((ROWS[1], 128), BF16),
+            *[shape((rows, 128), BF16) for rows in ROWS],
         ),
         in_specs=[HBM] * 9,
-        out_specs=(VMEM,) * 4,
+        out_specs=(VMEM,) * 5,
         scratch_shapes=[
             *[pltpu.VMEM(arg.shape, arg.dtype) for arg in args], sem((9,)),
             pltpu.VMEM((PACKED, PAIR), BF16),
@@ -502,10 +538,8 @@
             pltpu.VMEM((4, PACKED, 2 * C), BF16),
             pltpu.VMEM((4, PACKED - STAY, 2 * C), BF16),
             sem((4, 3)), sem((4, 3)),
-            pltpu.VMEM((ROWS[0], 128), BF16),
-            pltpu.VMEM((ROWS[1], 128), BF16),
-            *sum_bufs(CHUNK[0]), *sum_bufs(CHUNK[1]),
-            *sum_sems(), *sum_sems(),
+            *[pltpu.VMEM((rows, 128), BF16) for rows in ROWS],
+            *[ref for kind, size in PARTS for ref in sum_scratch(kind, size)],
         ],
         compiler_params=pltpu.CompilerParams(
             collective_id=0, has_side_effects=True, vmem_limit_bytes=56 * 2**20
@@ -515,13 +549,13 @@
 
 
 def finish_kernel(
-    out_hbm, gx_hbm, full0_hbm, full1_hbm, wqkv_hbm, wup_hbm, gain_a_hbm, gain_m_hbm,
+    out_hbm, gx_hbm, full0_hbm, full1_hbm, full2_hbm, wqkv_hbm, wup_hbm, gain_a_hbm, gain_m_hbm,
     out_ref, gx_ref, qkv_ref, proj_ref, up_ref, down_ref, ga_ref, gm_ref,
-    full0, full1, wqkv, wup, gain_a, gain_m, sem,
+    full0, full1, full2, wqkv, wup, gain_a, gain_m, sem,
 ):
     copies = []
     for i, (src, dst) in enumerate((
-        (full1_hbm, full1), (full0_hbm, full0), (wqkv_hbm, wqkv), (wup_hbm, wup),
+        (full0_hbm, full0), (full1_hbm, full1), (full2_hbm, full2), (wqkv_hbm, wqkv), (wup_hbm, wup),
         (gain_a_hbm, gain_a), (gain_m_hbm, gain_m), (out_hbm, out_ref), (gx_hbm, gx_ref),
     )):
         copies.append(pltpu.make_async_copy(src, dst, sem.at[i]))
@@ -530,18 +564,18 @@
     def block(full, t):
         return full[t * C:(t + 1) * C, :].astype(F32) * FACTOR
 
-    copies[0].wait()
-    copies[1].wait()
+    for copy in copies[:3]:
+        copy.wait()
     for t in range(4):
-        qkv_ref[:, t * 128:(t + 1) * 128] = block(full1, t)
-    mixed_tile = block(full1, 4)
+        qkv_ref[:, t * 128:(t + 1) * 128] = block(full2, t)
+    mixed_tile = block(full2, 4)
     qkv_ref[:, 512:] = mixed_tile[:, :64]
-    proj_ref[:, :128] = block(full0, 12)
+    proj_ref[:, :128] = block(full0, 6)
     proj_ref[:, 128:] = mixed_tile[:, 64:]
     for t in range(6):
-        up_ref[:, t * 128:(t + 1) * 128] = block(full0, t)
-        down_ref[:, t * 128:(t + 1) * 128] = block(full0, 6 + t)
-    for copy in copies[2:]:
+        up_ref[:, t * 128:(t + 1) * 128] = block(full1, t) if t < 5 else block(full0, 7)
+        down_ref[:, t * 128:(t + 1) * 128] = block(full0, t)
+    for copy in copies[3:]:
         copy.wait()
     for weight, grad, gain, ref in ((wqkv, qkv_ref, gain_a, ga_ref), (wup, up_ref, gain_m, gm_ref)):
         product = weight[...].astype(F32) * grad[...]
@@ -552,7 +586,7 @@
         ref[...] = total[:1] / gain[...]
 
 
-def finish_call(out, gx, full0, full1, w_qkv, w_up, gain_attn, gain_mlp):
+def finish_call(out, gx, full, w_qkv, w_up, gain_attn, gain_mlp):
     shape = jax.ShapeDtypeStruct
     return pl.pallas_call(
         finish_kernel,
@@ -566,29 +600,28 @@
             shape((1, C), F32),
             shape((1, C), F32),
         ),
-        in_specs=[HBM] * 8,
+        in_specs=[HBM] * 9,
         out_specs=(VMEM,) * 8,
         scratch_shapes=[
-            pltpu.VMEM((ROWS[0], 128), BF16),
-            pltpu.VMEM((ROWS[1], 128), BF16),
+            *[pltpu.VMEM((rows, 128), BF16) for rows in ROWS],
             pltpu.VMEM((C, 3 * C), BF16),
             pltpu.VMEM((C, FF), BF16),
             pltpu.VMEM((1, C), F32),
             pltpu.VMEM((1, C), F32),
-            pltpu.SemaphoreType.DMA((8,)),
+            pltpu.SemaphoreType.DMA((9,)),
         ],
         compiler_params=pltpu.CompilerParams(vmem_limit_bytes=56 * 2**20),
         name="finish",
-    )(out, gx, full0, full1, w_qkv, w_up, gain_attn, gain_mlp)
+    )(out, gx, *full, w_qkv, w_up, gain_attn, gain_mlp)
 
 
 def body(fields, gain_attn, w_qkv, bias, w_proj, gain_mlp, w_up, w_down, cotangent):
-    out, gx, full0, full1 = block_call(
+    out, gx, *full = block_call(
         fields.reshape(TOK, C), cotangent.reshape(TOK, C), bias.reshape(HEADS * WTOK, WTOK),
         gain_attn.reshape(1, C), w_qkv, w_proj, gain_mlp.reshape(1, C), w_up, w_down.T,
     )
     out, gx, qkv, proj, up, down, ga, gm = finish_call(
-        out, gx, full0, full1, w_qkv, w_up, gain_attn.reshape(1, C), gain_mlp.reshape(1, C),
+        out, gx, full, w_qkv, w_up, gain_attn.reshape(1, C), gain_mlp.reshape(1, C),
     )
     return (
         out.reshape(fields.shape), gx.reshape(fields.shape), qkv, proj, up, down.T,

time: 57.4 us -> 57.7 us (level)
  no operation moved by 1% of the time
where the time goes in v4:
time: 57.7 us; the launch traced here: 57.6 us
  Pallas kernels  56.8 us (98%)
  between operations  0.8 us (1%)
    pallas_call x1, Pallas kernels, block_call(): pl.pallas_call(block_kernel, out_shape=(shape((TOK, C), BF16), shape((TOK...  53.6 us
    pallas_call x1, Pallas kernels, finish_call(): pl.pallas_call(finish_kernel, out_shape=(shape((TOK, C), BF16), shape((TO...  3.22 us

profile of v4, /device:TPU:1, one launch (start us, length us, event | category | flops | bytes accessed | tf_op | source)
XLA Modules:
  0.0 57.6 jit_solution(16178309775176025701)
XLA Ops:
  0.6 53.6 %block.1 = (bf16[576,192]{1,0:T(8,128)(2,1)}, bf16[576,192]{1,0:T(8,128)(2,1)}, bf16[1536,128]{1,0:T(8,128)(2,1)}, bf16[1024,128]{1,0:T(8,128)(2,1)}, bf16[1024,128]{1,0:T(8,128)(2,1)}) custom-call(bf16[576,192]{1,0:T(8,128)(2,1)} %bitcast.12, bf16[576,192]{1,0:T(8,128)(2,1)} %bitcast.13, bf16[864,144]{1,0:T(8,128)(2,1)} %bitcast.11, f32[1,192]{1,0:T(1,128)} %bitcast.15, ...), custom_call_target="tpu_custom_call" | custom-call | tf_op jit(solution)/shard_map/block/pallas_call | solution.py:507
  54.2 3.2 %finish.1 = (bf16[576,192]{1,0:T(8,128)(2,1)}, bf16[576,192]{1,0:T(8,128)(2,1)}, f32[192,576]{1,0:T(8,128)}, f32[192,192]{1,0:T(8,128)}, f32[192,768]{1,0:T(8,12...) custom-call(bf16[576,192]{1,0:T(8,128)(2,1)} %get-tuple-element.21.out_hbm, ...), custom_call_target="tpu_custom_call" | custom-call | tf_op jit(solution)/shard_map/finish/pallas_call | solution.py:591

commit v5 on v4

--- a/solution.py
+++ b/solution.py
@@ -147,7 +147,7 @@
         return (self.lon, lat), (lon, self.lat), (lon, lat)
 
     def everyone(self):
-        devices = list(self.halo_targets(1)) + list(self.halo_targets(-1)) + [self.other_core()]
+        devices = list(self.halo_targets(-1)) + list(self.halo_targets(1)) + [self.other_core()]
         devices += [self.plane_peer(dy, dx) for dy, dx in PLANE]
         return devices + [self.z_peer(dz) for dz in range(1, 8)]
 
@@ -187,15 +187,15 @@
     def __init__(self, spot, flat, full, scratch):
         self.spot, self.flat, self.full = spot, flat, full
         (self.core_in, self.out, self.first_in, self.second_in, core, first_s, first_r,
-         second_s, second_r, back_s, back_r, last_s, last_r) = scratch
+         second_s, second_r, back_s, back_r, last) = scratch
         self.core_sems = core.at[0], core.at[1]
         self.first_sems, self.second_sems = (first_s, first_r), (second_s, second_r)
-        self.back_sems, self.last_sems = (back_s, back_r), (last_s, last_r)
+        self.back_sems, self.last_sems = (back_s, back_r), (last.at[0], last.at[1])
         self.size = self.first_in.shape[1]
         self.sent = []
         self.count = self.first_in.shape[0] + 1
         self.half = spot.core * (self.count * self.size)
-        self.own = self.first_index(self.first_steps[-1], True) * self.size
+        self.own = self.first_here() * self.size
 
     def launch(self, src, dst, sems, device, index=None):
         send_sem, recv_sem = sems if index is None else (sems[0].at[index], sems[1].at[index])
@@ -248,20 +248,13 @@
         ))
 
     def back_to_core(self):
-        self.last_copies = []
-        for k in range(self.count):
-            start = self.own
-            if k > 0:
-                self.back_copies[k - 1].wait_recv()
-                start = self.first_index(self.first_steps[k - 1], False, -1) * self.size
-            rows = self.full.at[chunk(self.half + start, self.size)]
-            self.last_copies.append(
-                self.launch(rows, rows, self.last_sems, self.spot.other_core(), k)
-            )
+        for copy in self.back_copies:
+            copy.wait_recv()
+        rows = self.full.at[chunk(self.half, self.count * self.size)]
+        self.last_copy = self.launch(rows, rows, self.last_sems, self.spot.other_core())
 
     def finish(self):
-        for copy in self.last_copies:
-            copy.wait_recv()
+        self.last_copy.wait_recv()
 
     def drain(self):
         for copy in self.sent:
@@ -271,8 +264,11 @@
 class PlaneSum(Sum):
     first_steps, second_steps = PLANE, RING
 
-    def first_index(self, step, here=False, sign=1):
-        y, x = (self.spot.y, self.spot.x) if here else self.spot.plane_spot(sign * step[0], sign * step[1])
+    def first_here(self):
+        return self.spot.y * 4 + self.spot.x
+
+    def first_index(self, step):
+        y, x = self.spot.plane_spot(*step)
         return y * 4 + x
 
     def first_peer(self, step):
@@ -288,8 +284,11 @@
 class RingSum(Sum):
     first_steps, second_steps = RING, PLANE
 
-    def first_index(self, step, here=False, sign=1):
-        return self.spot.z if here else ring(self.spot.z, sign * step, 8)
+    def first_here(self):
+        return self.spot.z
+
+    def first_index(self, step):
+        return ring(self.spot.z, step, 8)
 
     def first_peer(self, step):
         return self.spot.z_peer(step)
@@ -310,7 +309,7 @@
         pltpu.VMEM((first, size, 128), BF16),
         pltpu.VMEM((second + 1, size, 128), BF16),
         sem((2,)), sem((first,)), sem((first,)), sem((second,)), sem((second,)),
-        sem((first,)), sem((first,)), sem((first + 1,)), sem((first + 1,)),
+        sem((first,)), sem((first,)), sem((2,)),
     ]
 
 
@@ -322,11 +321,15 @@
     out_grid, gx_grid, full0, full1, full2,
     x_in, ct_in, bias_in, ga_in, wqkv_in, wproj_in, gm_in, wup_in, wdown_in, load_sem,
     pack, pack_t, place, place_t,
-    x_ref, ct_ref, out_ref, gx_ref, bias32, probs,
-    normed_s, qkv_s, mixed_s, hid_s, hid_grad_s, nm_s, act_s, gpre_s, gqkv_s, gattn_s,
+    x_ref, ct_ref, out_ref, gx_ref, bias32, probs, weights, km_s, vm_s, q_s,
+    normed_t, nm_t, mixed_t, ct_t, mixed_s, hid_s, hid_grad_s, nm_s, act_s, gpre_s, gqkv_s, gattn_s,
     packed, landed, halo_send, halo_recv, flat0, flat1, flat2, *sum_refs,
 ):
     spot = Place()
+    barrier = pltpu.get_barrier_semaphore()
+    devices = spot.everyone()
+    for device in devices[:6]:
+        pl.semaphore_signal(barrier, inc=1, device_id=device, device_id_type=MESH)
     loads = []
     for i, (src, dst) in enumerate((
         (x_hbm, x_in), (ct_hbm, ct_in), (bias_hbm, bias_in), (ga_hbm, ga_in), (wqkv_hbm, wqkv_in),
@@ -334,9 +337,7 @@
     )):
         loads.append(pltpu.make_async_copy(src, dst, load_sem.at[i]))
         loads[-1].start()
-    barrier = pltpu.get_barrier_semaphore()
-    devices = spot.everyone()
-    for device in devices:
+    for device in devices[6:]:
         pl.semaphore_signal(barrier, inc=1, device_id=device, device_id_type=MESH)
     halos = [
         Halo(spot, packed.at[a], landed.at[a], halo_send.at[a], halo_recv.at[a], step)
@@ -385,29 +386,31 @@
     def forward():
         x = x_ref[...].astype(F32)
         unit, _ = normalize(x)
-        normed_s[...] = (unit * ga).astype(BF16)
-        qkv_s[...] = nn(normed_s[...], wqkv_in[...]).astype(BF16)
+        normed = (unit * ga).astype(BF16)
+        normed_t[...] = normed.T
+        qkv = nn(normed, wqkv_in[...]).astype(BF16)
+        q_s[...] = qkv[:, :C]
+        k = qkv[:, C:2 * C]
+        v = qkv[:, 2 * C:]
         for n in range(4):
             rows = slice(n * WTOK, (n + 1) * WTOK)
-            q, k, v = split_heads(rows)
-            km = jnp.concatenate([k * masks[h] for h in range(HEADS)], axis=0)
-            vm = jnp.concatenate([v * masks[h] for h in range(HEADS)], axis=0)
-            s = (nt(km, q) * scale + bias32[...]).reshape(HEADS, WTOK, WTOK)
+            km = jnp.concatenate([k[rows] * masks[h] for h in range(HEADS)], axis=0)
+            vm = jnp.concatenate([v[rows] * masks[h] for h in range(HEADS)], axis=0)
+            km_s[n] = km
+            vm_s[n] = vm
+            s = (nt(km, q_s[rows, :]) * scale + bias32[...]).reshape(HEADS, WTOK, WTOK)
             e = jnp.exp(s - jnp.max(s, axis=1, keepdims=True))
             p = e * (1.0 / jnp.sum(e, axis=1, keepdims=True))
             probs[n * HEADS:(n + 1) * HEADS] = p
-            mixed = tn(p.astype(BF16).reshape(HEADS * WTOK, WTOK), vm)
-            mixed_s[rows, :] = mixed.astype(BF16)
-
-    def split_heads(rows):
-        qkv = qkv_s[rows, :]
-        return qkv[:, :C], qkv[:, C:2 * C], qkv[:, 2 * C:]
+            weights[n] = p.astype(BF16).reshape(HEADS * WTOK, WTOK)
+            mixed_s[rows, :] = tn(weights[n], vm).astype(BF16)
 
     def mlp():
         hidden = (x_ref[...].astype(F32) + nn(mixed_s[...], wproj_in[...])).astype(BF16)
         hid_s[...] = hidden
         unit, inv = normalize(hidden.astype(F32))
         nm_s[...] = (unit * gm).astype(BF16)
+        nm_t[...] = nm_s[...].T
         grad_nm = jnp.zeros((TOK, C), F32)
         for f in range(3):
             cols = slice(f * 256, (f + 1) * 256)
@@ -424,17 +427,14 @@
 
     def attention_back(n):
         rows = slice(n * WTOK, (n + 1) * WTOK)
-        q, k, v = split_heads(rows)
         up = gattn_s[rows, :]
-        km = jnp.concatenate([k * masks[h] for h in range(HEADS)], axis=0)
-        vm = jnp.concatenate([v * masks[h] for h in range(HEADS)], axis=0)
         p = probs[n * HEADS:(n + 1) * HEADS]
-        gp = nt(vm, up).reshape(HEADS, WTOK, WTOK)
+        gp = nt(vm_s[n], up).reshape(HEADS, WTOK, WTOK)
         inner = jnp.sum(p * gp, axis=1, keepdims=True)
         gs = (p * (gp - inner) * scale).astype(BF16).reshape(HEADS * WTOK, WTOK)
-        gv_all = nn(p.astype(BF16).reshape(HEADS * WTOK, WTOK), up)
-        gk_all = nn(gs, q)
-        gq = tn(gs, km)
+        gv_all = nn(weights[n], up)
+        gk_all = nn(gs, q_s[rows, :])
+        gq = tn(gs, km_s[n])
         gk = jnp.zeros((WTOK, C), F32)
         gv = jnp.zeros((WTOK, C), F32)
         for h in range(HEADS):
@@ -456,13 +456,15 @@
             flat[base + t * C:base + (t + 1) * C, :] = values[:, t * 128:(t + 1) * 128].astype(BF16)
 
     forward()
+    mixed_t[...] = mixed_s[...].T
     ct_halo.wait()
     ct_halo.unpack(place_t, ct_ref)
+    ct_t[...] = ct_ref[...].T
     mlp()
-    grad_up = tn(nm_s[...], gpre_s[...])
-    grad_proj = tn(mixed_s[...], hid_grad_s[...])
+    grad_up = nn(nm_t[...], gpre_s[...])
+    grad_proj = nn(mixed_t[...], hid_grad_s[...])
     store_blocks(flat1, 0, grad_up[:, :640])
-    store_blocks(flat0, 0, tn(ct_ref[...], act_s[...]))
+    store_blocks(flat0, 0, nn(ct_t[...], act_s[...]))
     store_blocks(flat0, 6 * C, grad_proj)
     store_blocks(flat0, 7 * C, grad_up[:, 640:])
     for part in early:
@@ -473,13 +475,13 @@
         part.to_first()
     attention_back(2)
     attention_back(3)
-    grad_qkv = tn(normed_s[...], gqkv_s[...])
+    grad_qkv = nn(normed_t[...], gqkv_s[...])
     store_blocks(flat2, 0, grad_qkv)
     store_blocks(flat2, 4 * C, jnp.concatenate([grad_qkv[:, 512:], grad_proj[:, 128:]], axis=1))
     late.to_core()
+    late.to_first()
     output()
     out_halo.pack(out_ref, place)
-    late.to_first()
     input_grad()
     gx_halo.pack(gx_ref, place)
     out_halo.start()
@@ -525,8 +527,11 @@
             pltpu.VMEM((TOK, C), BF16),
             pltpu.VMEM((HEADS * WTOK, WTOK), F32),
             pltpu.VMEM((4 * HEADS, WTOK, WTOK), F32),
-            pltpu.VMEM((TOK, C), BF16),
-            pltpu.VMEM((TOK, 3 * C), BF16),
+            pltpu.VMEM((4, HEADS * WTOK, WTOK), BF16),
+            pltpu.VMEM((4, HEADS * WTOK, C), BF16),
+            pltpu.VMEM((4, HEADS * WTOK, C), BF16),
+            pltpu.VMEM((TOK, C), BF16),
+            *[pltpu.VMEM((C, TOK), BF16)] * 4,
             pltpu.VMEM((TOK, C), BF16),
             pltpu.VMEM((TOK, C), BF16),
             pltpu.VMEM((TOK, C), BF16),
@@ -549,33 +554,54 @@
 
 
 def finish_kernel(
-    out_hbm, gx_hbm, full0_hbm, full1_hbm, full2_hbm, wqkv_hbm, wup_hbm, gain_a_hbm, gain_m_hbm,
-    out_ref, gx_ref, qkv_ref, proj_ref, up_ref, down_ref, ga_ref, gm_ref,
-    full0, full1, full2, wqkv, wup, gain_a, gain_m, sem,
+    out_in, gx_in, full0_hbm, full1_hbm, full2_hbm, wqkv_hbm, wup_hbm, gain_a_hbm, gain_m_hbm,
+    out_hbm, gx_hbm, qkv_hbm, proj_hbm, up_hbm, down_hbm, ga_hbm, gm_hbm,
+    full0, full1, full2, wqkv, wup, gain_a, gain_m,
+    out_ref, gx_ref, qkv_ref, proj_ref, up_ref, down_ref, ga_ref, gm_ref, in_sem, out_sem,
 ):
-    copies = []
-    for i, (src, dst) in enumerate((
-        (full0_hbm, full0), (full1_hbm, full1), (full2_hbm, full2), (wqkv_hbm, wqkv), (wup_hbm, wup),
-        (gain_a_hbm, gain_a), (gain_m_hbm, gain_m), (out_hbm, out_ref), (gx_hbm, gx_ref),
-    )):
-        copies.append(pltpu.make_async_copy(src, dst, sem.at[i]))
-        copies[-1].start()
+    def read(i, src, dst):
+        copy = pltpu.make_async_copy(src, dst, in_sem.at[i])
+        copy.start()
+        return copy
+
+    written = []
+
+    def write(i, src, dst):
+        written.append(pltpu.make_async_copy(src, dst, out_sem.at[i]))
+        written[-1].start()
 
     def block(full, t):
         return full[t * C:(t + 1) * C, :].astype(F32) * FACTOR
 
-    for copy in copies[:3]:
-        copy.wait()
+    copies = [
+        read(i, src, dst) for i, (src, dst) in enumerate((
+            (full0_hbm, full0), (full1_hbm, full1), (full2_hbm, full2), (out_in, out_ref),
+            (gx_in, gx_ref), (wqkv_hbm, wqkv), (wup_hbm, wup), (gain_a_hbm, gain_a),
+            (gain_m_hbm, gain_m),
+        ))
+    ]
+    copies[0].wait()
+    for t in range(6):
+        down_ref[:, t * 128:(t + 1) * 128] = block(full0, t)
+    write(0, down_ref, down_hbm)
+    copies[1].wait()
+    for t in range(6):
+        up_ref[:, t * 128:(t + 1) * 128] = block(full1, t) if t < 5 else block(full0, 7)
+    write(1, up_ref, up_hbm)
+    copies[2].wait()
     for t in range(4):
         qkv_ref[:, t * 128:(t + 1) * 128] = block(full2, t)
     mixed_tile = block(full2, 4)
     qkv_ref[:, 512:] = mixed_tile[:, :64]
+    write(2, qkv_ref, qkv_hbm)
     proj_ref[:, :128] = block(full0, 6)
     proj_ref[:, 128:] = mixed_tile[:, 64:]
-    for t in range(6):
-        up_ref[:, t * 128:(t + 1) * 128] = block(full1, t) if t < 5 else block(full0, 7)
-        down_ref[:, t * 128:(t + 1) * 128] = block(full0, t)
-    for copy in copies[3:]:
+    write(3, proj_ref, proj_hbm)
+    copies[3].wait()
+    write(4, out_ref, out_hbm)
+    copies[4].wait()
+    write(5, gx_ref, gx_hbm)
+    for copy in copies[5:]:
         copy.wait()
     for weight, grad, gain, ref in ((wqkv, qkv_ref, gain_a, ga_ref), (wup, up_ref, gain_m, gm_ref)):
         product = weight[...].astype(F32) * grad[...]
@@ -584,31 +610,38 @@
             precision=lax.Precision.HIGHEST, preferred_element_type=F32,
         )
         ref[...] = total[:1] / gain[...]
+    write(6, ga_ref, ga_hbm)
+    write(7, gm_ref, gm_hbm)
+    for copy in written:
+        copy.wait()
 
 
 def finish_call(out, gx, full, w_qkv, w_up, gain_attn, gain_mlp):
     shape = jax.ShapeDtypeStruct
+    results = (
+        shape((TOK, C), BF16),
+        shape((TOK, C), BF16),
+        shape((C, 3 * C), F32),
+        shape((C, C), F32),
+        shape((C, FF), F32),
+        shape((C, FF), F32),
+        shape((1, C), F32),
+        shape((1, C), F32),
+    )
     return pl.pallas_call(
         finish_kernel,
-        out_shape=(
-            shape((TOK, C), BF16),
-            shape((TOK, C), BF16),
-            shape((C, 3 * C), F32),
-            shape((C, C), F32),
-            shape((C, FF), F32),
-            shape((C, FF), F32),
-            shape((1, C), F32),
-            shape((1, C), F32),
-        ),
+        out_shape=results,
         in_specs=[HBM] * 9,
-        out_specs=(VMEM,) * 8,
+        out_specs=(HBM,) * 8,
         scratch_shapes=[
             *[pltpu.VMEM((rows, 128), BF16) for rows in ROWS],
             pltpu.VMEM((C, 3 * C), BF16),
             pltpu.VMEM((C, FF), BF16),
             pltpu.VMEM((1, C), F32),
             pltpu.VMEM((1, C), F32),
+            *[pltpu.VMEM(result.shape, result.dtype) for result in results],
             pltpu.SemaphoreType.DMA((9,)),
+            pltpu.SemaphoreType.DMA((8,)),
         ],
         compiler_params=pltpu.CompilerParams(vmem_limit_bytes=56 * 2**20),
         name="finish",

time: 57.7 us -> 58.5 us (1.014)
  Pallas kernels: 56.8 us -> 57.5 us
    pallas_call x1, Pallas kernels: 53.6 us -> 54.3 us  [block_call(): pl.pallas_call(block_kernel, out_shape=(shape((TOK, C), BF16), shape((TOK...]
where the time goes in v5:
time: 58.5 us; the launch traced here: 58.3 us
  Pallas kernels  57.5 us (98%)
  between operations  0.8 us (1%)
    pallas_call x1, Pallas kernels, block_call(): pl.pallas_call(block_kernel, out_shape=(shape((TOK, C), BF16), shape((TOK...  54.3 us
    pallas_call x1, Pallas kernels, finish_call(): pl.pallas_call(finish_kernel, out_shape=results, in_specs=[HBM] * 9, out_...  3.26 us

profile of v5, /device:TPU:1, one launch (start us, length us, event | category | flops | bytes accessed | tf_op | source)
XLA Modules:
  0.0 58.3 jit_solution(342124094329892289)
XLA Ops:
  0.6 54.3 %block.1 = (bf16[576,192]{1,0:T(8,128)(2,1)}, bf16[576,192]{1,0:T(8,128)(2,1)}, bf16[1536,128]{1,0:T(8,128)(2,1)}, bf16[1024,128]{1,0:T(8,128)(2,1)}, bf16[1024,128]{1,0:T(8,128)(2,1)}) custom-call(bf16[576,192]{1,0:T(8,128)(2,1)} %bitcast.12, bf16[576,192]{1,0:T(8,128)(2,1)} %bitcast.13, bf16[864,144]{1,0:T(8,128)(2,1)} %bitcast.11, f32[1,192]{1,0:T(1,128)} %bitcast.15, ...), custom_call_target="tpu_custom_call" | custom-call | tf_op jit(solution)/shard_map/block/pallas_call | solution.py:509
  54.9 3.3 %finish.1 = (bf16[576,192]{1,0:T(8,128)(2,1)}, bf16[576,192]{1,0:T(8,128)(2,1)}, f32[192,576]{1,0:T(8,128)}, f32[192,192]{1,0:T(8,128)}, f32[192,768]{1,0:T(8,12...) custom-call(bf16[576,192]{1,0:T(8,128)(2,1)} %get-tuple-element.21.out_in, ...), custom_call_target="tpu_custom_call" | custom-call | tf_op jit(solution)/shard_map/finish/pallas_call | solution.py:631

commit v6 on v5

--- a/solution.py
+++ b/solution.py
@@ -484,18 +484,18 @@
     out_halo.pack(out_ref, place)
     input_grad()
     gx_halo.pack(gx_ref, place)
-    out_halo.start()
-    gx_halo.start()
     for part in sums:
         part.to_second()
+    out_halo.start()
+    for part in sums:
+        part.back_to_first()
+    gx_halo.start()
     out_halo.wait()
     out_halo.unpack(pack_t, out_grid)
     for part in sums:
-        part.back_to_first()
+        part.back_to_core()
     gx_halo.wait()
     gx_halo.unpack(pack_t, gx_grid)
-    for part in sums:
-        part.back_to_core()
     for part in sums:
         part.finish()
     for part in sums:

time: 58.5 us -> 54.4 us (0.930)
  Pallas kernels: 57.5 us -> 53.5 us
    pallas_call x1, Pallas kernels: 54.3 us -> 50.3 us  [block_call(): pl.pallas_call(block_kernel, out_shape=(shape((TOK, C), BF16), shape((TOK...]
where the time goes in v6:
time: 54.4 us; the launch traced here: 54.3 us
  Pallas kernels  53.5 us (98%)
  between operations  0.8 us (1%)
    pallas_call x1, Pallas kernels, block_call(): pl.pallas_call(block_kernel, out_shape=(shape((TOK, C), BF16), shape((TOK...  50.3 us
    pallas_call x1, Pallas kernels, finish_call(): pl.pallas_call(finish_kernel, out_shape=results, in_specs=[HBM] * 9, out_...  3.26 us

profile of v6, /device:TPU:1, one launch (start us, length us, event | category | flops | bytes accessed | tf_op | source)
XLA Modules:
  0.0 54.3 jit_solution(16958493046889006180)
XLA Ops:
  0.6 50.3 %block.1 = (bf16[576,192]{1,0:T(8,128)(2,1)}, bf16[576,192]{1,0:T(8,128)(2,1)}, bf16[1536,128]{1,0:T(8,128)(2,1)}, bf16[1024,128]{1,0:T(8,128)(2,1)}, bf16[1024,128]{1,0:T(8,128)(2,1)}) custom-call(bf16[576,192]{1,0:T(8,128)(2,1)} %bitcast.12, bf16[576,192]{1,0:T(8,128)(2,1)} %bitcast.13, bf16[864,144]{1,0:T(8,128)(2,1)} %bitcast.11, f32[1,192]{1,0:T(1,128)} %bitcast.15, ...), custom_call_target="tpu_custom_call" | custom-call | tf_op jit(solution)/shard_map/block/pallas_call | solution.py:509
  50.9 3.3 %finish.1 = (bf16[576,192]{1,0:T(8,128)(2,1)}, bf16[576,192]{1,0:T(8,128)(2,1)}, f32[192,576]{1,0:T(8,128)}, f32[192,192]{1,0:T(8,128)}, f32[192,768]{1,0:T(8,12...) custom-call(bf16[576,192]{1,0:T(8,128)(2,1)} %get-tuple-element.21.out_in, ...), custom_call_target="tpu_custom_call" | custom-call | tf_op jit(solution)/shard_map/finish/pallas_call | solution.py:631

commit v7 on v6

--- a/solution.py
+++ b/solution.py
@@ -168,9 +168,17 @@
         for copy in self.copies:
             copy.start()
 
+    def wait_sent(self):
+        for copy in self.copies:
+            copy.wait_send()
+
+    def wait_landed(self):
+        for copy in self.copies:
+            copy.wait_recv()
+
     def wait(self):
-        for copy in self.copies:
-            copy.wait()
+        self.wait_sent()
+        self.wait_landed()
 
     def pack(self, ref, table_ref):
         pairs = [ref[i * PAIR:(i + 1) * PAIR, :].astype(F32) for i in range(2)]
@@ -363,7 +371,6 @@
     place_t[...] = table_t(place_rows)
     loads[1].wait()
     ct_halo.pack(ct_in, pack)
-    ct_halo.start()
     loads[2].wait()
     is_last = spot.lat == lax.axis_size("lat") - 1
     row_half = (lax.broadcasted_iota(jnp.int32, (WTOK, 1), 0) // WLON) % WLAT < WLAT // 2
@@ -375,7 +382,9 @@
         bias32[rows, :] = bias_in[rows, :].astype(F32).T + penalty
     for load in loads[3:]:
         load.wait()
-    x_halo.wait()
+    x_halo.wait_sent()
+    ct_halo.start()
+    x_halo.wait_landed()
     x_halo.unpack(place_t, x_ref)
 
     scale = HEAD ** (-0.5)
@@ -482,14 +491,14 @@
     late.to_first()
     output()
     out_halo.pack(out_ref, place)
+    out_halo.start()
     input_grad()
     gx_halo.pack(gx_ref, place)
     for part in sums:
         part.to_second()
-    out_halo.start()
+    gx_halo.start()
     for part in sums:
         part.back_to_first()
-    gx_halo.start()
     out_halo.wait()
     out_halo.unpack(pack_t, out_grid)
     for part in sums:

time: 54.4 us -> 54.7 us (level)
  no operation moved by 1% of the time
where the time goes in v7:
time: 54.7 us; the launch traced here: 54.5 us
  Pallas kernels  53.7 us (98%)
  between operations  0.8 us (1%)
    pallas_call x1, Pallas kernels, block_call(): pl.pallas_call(block_kernel, out_shape=(shape((TOK, C), BF16), shape((TOK...  50.5 us
    pallas_call x1, Pallas kernels, finish_call(): pl.pallas_call(finish_kernel, out_shape=results, in_specs=[HBM] * 9, out_...  3.26 us

profile of v7, /device:TPU:1, one launch (start us, length us, event | category | flops | bytes accessed | tf_op | source)
XLA Modules:
  0.0 54.5 jit_solution(6335025452758907485)
XLA Ops:
  0.6 50.5 %block.1 = (bf16[576,192]{1,0:T(8,128)(2,1)}, bf16[576,192]{1,0:T(8,128)(2,1)}, bf16[1536,128]{1,0:T(8,128)(2,1)}, bf16[1024,128]{1,0:T(8,128)(2,1)}, bf16[1024,128]{1,0:T(8,128)(2,1)}) custom-call(bf16[576,192]{1,0:T(8,128)(2,1)} %bitcast.12, bf16[576,192]{1,0:T(8,128)(2,1)} %bitcast.13, bf16[864,144]{1,0:T(8,128)(2,1)} %bitcast.11, f32[1,192]{1,0:T(1,128)} %bitcast.15, ...), custom_call_target="tpu_custom_call" | custom-call | tf_op jit(solution)/shard_map/block/pallas_call | solution.py:518
  51.1 3.3 %finish.1 = (bf16[576,192]{1,0:T(8,128)(2,1)}, bf16[576,192]{1,0:T(8,128)(2,1)}, f32[192,576]{1,0:T(8,128)}, f32[192,192]{1,0:T(8,128)}, f32[192,768]{1,0:T(8,12...) custom-call(bf16[576,192]{1,0:T(8,128)(2,1)} %get-tuple-element.21.out_in, ...), custom_call_target="tpu_custom_call" | custom-call | tf_op jit(solution)/shard_map/finish/pallas_call | solution.py:640

commit v8 on v5

--- a/solution.py
+++ b/solution.py
@@ -469,22 +469,20 @@
     store_blocks(flat0, 7 * C, grad_up[:, 640:])
     for part in early:
         part.to_core()
-    attention_back(0)
-    attention_back(1)
+    output()
+    out_halo.pack(out_ref, place)
     for part in early:
         part.to_first()
-    attention_back(2)
-    attention_back(3)
+    out_halo.start()
+    for n in range(4):
+        attention_back(n)
     grad_qkv = nn(normed_t[...], gqkv_s[...])
     store_blocks(flat2, 0, grad_qkv)
     store_blocks(flat2, 4 * C, jnp.concatenate([grad_qkv[:, 512:], grad_proj[:, 128:]], axis=1))
     late.to_core()
     late.to_first()
-    output()
-    out_halo.pack(out_ref, place)
     input_grad()
     gx_halo.pack(gx_ref, place)
-    out_halo.start()
     gx_halo.start()
     for part in sums:
         part.to_second()

time: 58.5 us -> 56.1 us (0.959)
  Pallas kernels: 57.5 us -> 55.2 us
    pallas_call x1, Pallas kernels: 54.3 us -> 51.9 us  [block_call(): pl.pallas_call(block_kernel, out_shape=(shape((TOK, C), BF16), shape((TOK...]
where the time goes in v8:
time: 56.1 us; the launch traced here: 56 us
  Pallas kernels  55.2 us (98%)
  between operations  0.8 us (1%)
    pallas_call x1, Pallas kernels, block_call(): pl.pallas_call(block_kernel, out_shape=(shape((TOK, C), BF16), shape((TOK...  51.9 us
    pallas_call x1, Pallas kernels, finish_call(): pl.pallas_call(finish_kernel, out_shape=results, in_specs=[HBM] * 9, out_...  3.26 us

profile of v8, /device:TPU:1, one launch (start us, length us, event | category | flops | bytes accessed | tf_op | source)
XLA Modules:
  0.0 56.0 jit_solution(17383971311798834877)
XLA Ops:
  0.6 51.9 %block.1 = (bf16[576,192]{1,0:T(8,128)(2,1)}, bf16[576,192]{1,0:T(8,128)(2,1)}, bf16[1536,128]{1,0:T(8,128)(2,1)}, bf16[1024,128]{1,0:T(8,128)(2,1)}, bf16[1024,128]{1,0:T(8,128)(2,1)}) custom-call(bf16[576,192]{1,0:T(8,128)(2,1)} %bitcast.12, bf16[576,192]{1,0:T(8,128)(2,1)} %bitcast.13, bf16[864,144]{1,0:T(8,128)(2,1)} %bitcast.11, f32[1,192]{1,0:T(1,128)} %bitcast.15, ...), custom_call_target="tpu_custom_call" | custom-call | tf_op jit(solution)/shard_map/block/pallas_call | solution.py:507
  52.6 3.3 %finish.1 = (bf16[576,192]{1,0:T(8,128)(2,1)}, bf16[576,192]{1,0:T(8,128)(2,1)}, f32[192,576]{1,0:T(8,128)}, f32[192,192]{1,0:T(8,128)}, f32[192,768]{1,0:T(8,12...) custom-call(bf16[576,192]{1,0:T(8,128)(2,1)} %get-tuple-element.21.out_in, ...), custom_call_target="tpu_custom_call" | custom-call | tf_op jit(solution)/shard_map/finish/pallas_call | solution.py:629

commit v9 on v6

--- a/solution.py
+++ b/solution.py
@@ -487,9 +487,9 @@
     for part in sums:
         part.to_second()
     out_halo.start()
+    gx_halo.start()
     for part in sums:
         part.back_to_first()
-    gx_halo.start()
     out_halo.wait()
     out_halo.unpack(pack_t, out_grid)
     for part in sums:

time: 54.4 us -> 55.6 us (1.022)
  Pallas kernels: 53.5 us -> 54.7 us
    pallas_call x1, Pallas kernels: 50.3 us -> 51.5 us  [block_call(): pl.pallas_call(block_kernel, out_shape=(shape((TOK, C), BF16), shape((TOK...]
where the time goes in v9:
time: 55.6 us; the launch traced here: 55.5 us
  Pallas kernels  54.7 us (98%)
  between operations  0.8 us (1%)
    pallas_call x1, Pallas kernels, block_call(): pl.pallas_call(block_kernel, out_shape=(shape((TOK, C), BF16), shape((TOK...  51.5 us
    pallas_call x1, Pallas kernels, finish_call(): pl.pallas_call(finish_kernel, out_shape=results, in_specs=[HBM] * 9, out_...  3.26 us

profile of v9, /device:TPU:1, one launch (start us, length us, event | category | flops | bytes accessed | tf_op | source)
XLA Modules:
  0.0 55.5 jit_solution(14575375702313480093)
XLA Ops:
  0.6 51.5 %block.1 = (bf16[576,192]{1,0:T(8,128)(2,1)}, bf16[576,192]{1,0:T(8,128)(2,1)}, bf16[1536,128]{1,0:T(8,128)(2,1)}, bf16[1024,128]{1,0:T(8,128)(2,1)}, bf16[1024,128]{1,0:T(8,128)(2,1)}) custom-call(bf16[576,192]{1,0:T(8,128)(2,1)} %bitcast.12, bf16[576,192]{1,0:T(8,128)(2,1)} %bitcast.13, bf16[864,144]{1,0:T(8,128)(2,1)} %bitcast.11, f32[1,192]{1,0:T(1,128)} %bitcast.15, ...), custom_call_target="tpu_custom_call" | custom-call | tf_op jit(solution)/shard_map/block/pallas_call | solution.py:509
  52.1 3.3 %finish.1 = (bf16[576,192]{1,0:T(8,128)(2,1)}, bf16[576,192]{1,0:T(8,128)(2,1)}, f32[192,576]{1,0:T(8,128)}, f32[192,192]{1,0:T(8,128)}, f32[192,768]{1,0:T(8,12...) custom-call(bf16[576,192]{1,0:T(8,128)(2,1)} %get-tuple-element.21.out_in, ...), custom_call_target="tpu_custom_call" | custom-call | tf_op jit(solution)/shard_map/finish/pallas_call | solution.py:631
